TPU v7x, 512 devices: a whole 4x8x8 slice. The times are simulated.
512 devices in a mesh: shot: 64 (over y_lo, z, core), rec: 8 (over y_hi, x).
Axes of the slice: x: 4, y: 8 (y_hi: 2, y_lo: 4; y = y_hi * 4 + y_lo), z: 8, core: 2. Of those that a mesh axis runs over, the one named last changes fastest.
Arguments:
- noisy: bfloat16 [1, 256, 32, 8, 512], P(None, 'shot', 'rec'), may hold values from -12 to 12
- misfit: bfloat16 [1, 256, 32, 8, 512], P(None, 'shot', 'rec'), may hold values from -48 to 48
- timestep: int32 [1], replicated, may hold values from 0 to 999
- segment_ids: int32 [256], replicated, may hold values from 0 to 41, never falling along the last dimension, each value on 1 to 12 neighbouring positions
- w_qkv: bfloat16 [2, 512, 1536], replicated, may hold values from -32 to 32
- w_out: bfloat16 [2, 512, 512], replicated, may hold values from -0.25 to 0.25
Outputs:
- denoised: bfloat16 [1, 256, 32, 8, 512], P(None, 'shot', 'rec')
- guidance: bfloat16 [1, 256, 32, 8, 512], P(None, 'shot', 'rec')
Inputs may be any that keep to these rules, and one draw needn't show every extreme that they name: `segment_ids`: the shot group of each shot token; never falls from one shot token to the next; each group covers 1 to 12 shot tokens.
All inputs are finite; a program needn't handle non-finite values.
Results may differ from a plain program's by a relative error of at most 0.03.
The roundings to bfloat16 on the way count: a program that leaves them out, or rounds other values in their place, can miss the bound.
Values may be sent and summed in bfloat16 or wider, within the bound.
A program may use at most 128 MiB of HBM per device.

v0:
```python
import math

import jax
import jax.numpy as jnp
from jax import lax
from jax.sharding import PartitionSpec as P

HEADS = 16
HS = 32
STEPS = 1000


sigma_low = 0.5
sigma_high = 8.0
sigma_data = 0.5
norm_eps = 1e-06
highest = lax.Precision.HIGHEST


def extended(x, sides, width):
    for axis, dim in sides:
        size, length = (lax.axis_size(axis), x.shape[dim])
        up = [(i, (i + 1) % size) for i in range(size)]
        down = [(j, i) for i, j in up]
        last = lax.slice_in_dim(x, length - width, length, axis=dim)
        first = lax.slice_in_dim(x, 0, width, axis=dim)
        before = lax.ppermute(last, axis, up)
        after = lax.ppermute(first, axis, down)
        x = jnp.concatenate([before, x, after], axis=dim)
    return x


def precondition(timestep):
    fraction = timestep[0].astype(jnp.float32) / (STEPS - 1)
    noise_level = sigma_low * jnp.exp(fraction * math.log(sigma_high / sigma_low))
    spread = noise_level * noise_level + sigma_data * sigma_data
    c_skip = sigma_data * sigma_data / spread
    c_out = noise_level * sigma_data * lax.rsqrt(spread)
    c_in = lax.rsqrt(spread)
    return (c_skip, c_out, c_in)


def line_ids(segment_ids, shot_index, rec_index, shifted, half_tok, time_tok):
    shot_part = jnp.take(segment_ids, shot_index) * 4
    if shifted:
        shot_part = shot_part + 2 * (shot_index < half_tok).astype(jnp.int32)
        rec_part = (rec_index < half_tok).astype(jnp.int32)
    else:
        rec_part = jnp.zeros(rec_index.shape, jnp.int32)
    ids = shot_part[:, None] + rec_part[None, :]
    return jnp.broadcast_to(ids[:, :, None], ids.shape + (time_tok,)).reshape(-1)


def window_layout(segment_ids, shifted, half_tok, time_tok):
    shot_pos = lax.axis_index("shot")
    rec_pos = lax.axis_index("rec")
    if shifted:
        shot_at = half_tok * (shot_pos % 2)
        rec_at = half_tok * (rec_pos % 2)
    else:
        shot_at = half_tok * (1 - shot_pos % 2)
        rec_at = half_tok * (1 - rec_pos % 2)
    shot_tokens = segment_ids.shape[0]
    rec_tokens = half_tok * lax.axis_size("rec")
    window_steps = jnp.arange(2 * half_tok, dtype=jnp.int32)
    own_steps = jnp.arange(half_tok, dtype=jnp.int32)
    window_shot = (half_tok * shot_pos - half_tok + shot_at + window_steps) % shot_tokens
    window_rec = (half_tok * rec_pos - half_tok + rec_at + window_steps) % rec_tokens
    own_shot = half_tok * shot_pos + own_steps
    own_rec = half_tok * rec_pos + own_steps
    window_line = line_ids(segment_ids, window_shot, window_rec, shifted, half_tok, time_tok)
    query_line = line_ids(segment_ids, own_shot, own_rec, shifted, half_tok, time_tok)
    return (shot_at, rec_at, query_line, window_line)


def window_region(source, shot_at, rec_at):
    edge = 2 * (source.shape[1] // 3)
    sizes = (source.shape[0], edge, edge, source.shape[3], source.shape[4])
    return lax.dynamic_slice(source, (0, shot_at, rec_at, 0, 0), sizes)


def heads_last(field):
    batches = field.shape[0]
    flat = field.reshape(batches, -1, HEADS, HS)
    return jnp.transpose(flat, (0, 2, 3, 1))


def tokens_last_back(heads, shape):
    return jnp.transpose(heads, (0, 3, 1, 2)).reshape(shape)


def pair_scores(left, right):
    return jnp.einsum(
        "bhdq,bhdk->bhqk", left, right, preferred_element_type=jnp.float32, precision=highest
    ) * HS ** (-0.5)


def log_totals(scores, allowed):
    row_max = jnp.max(jnp.where(allowed, scores, -jnp.inf), axis=-1)
    shifted_exp = jnp.where(allowed, jnp.exp(scores - row_max[..., None]), 0.0)
    return row_max + jnp.log(jnp.sum(shifted_exp, axis=-1))


def attention_of(scores, log_total, allowed):
    return jnp.where(allowed, jnp.exp(scores - log_total[..., None]), 0.0)


def block_ahead(stream, w_layer, w_proj, segment_ids, shifted):
    half_tok = stream.shape[1]
    time_tok = stream.shape[3]
    features = stream.shape[4]
    inverse = lax.rsqrt(jnp.mean(stream * stream, axis=-1, keepdims=True) + norm_eps)
    normed = (stream * inverse).astype(jnp.bfloat16)
    shot_at, rec_at, query_line, window_line = window_layout(
        segment_ids, shifted, half_tok, time_tok
    )
    packed = jnp.dot(normed, w_layer, preferred_element_type=jnp.float32)
    queries = packed[..., :features]
    neighbours = extended(packed[..., features:], (("shot", 1), ("rec", 2)), half_tok)
    window_kv = window_region(neighbours, shot_at, rec_at)
    allowed = (query_line[:, None] == window_line[None, :])[None, None, :, :]
    key_heads = heads_last(window_kv[..., :features])
    value_heads = heads_last(window_kv[..., features:])
    scores = pair_scores(heads_last(queries), key_heads)
    log_total = log_totals(scores, allowed)
    attention = attention_of(scores, log_total, allowed).astype(jnp.bfloat16)
    attended = jnp.einsum(
        "bhqk,bhdk->bhdq",
        attention,
        value_heads,
        preferred_element_type=jnp.float32,
        precision=highest,
    )
    attended = tokens_last_back(attended, stream.shape).astype(jnp.bfloat16)
    branch = jnp.dot(attended, w_proj, preferred_element_type=jnp.float32)
    saved = (
        stream,
        inverse,
        queries,
        window_kv,
        log_total,
        shot_at,
        rec_at,
        query_line,
        window_line,
    )
    return (stream + branch, saved)


def block_back(grad_next, saved, w_layer, w_proj):
    stream, inverse, queries, window_kv, log_total, shot_at, rec_at, query_line, window_line = saved
    batches = stream.shape[0]
    half_tok = stream.shape[1]
    time_tok = stream.shape[3]
    features = stream.shape[4]
    contract = (((4,), (1,)), ((), ()))
    grad_attended = lax.dot_general(
        grad_next.astype(jnp.bfloat16), w_proj, contract, preferred_element_type=jnp.float32
    )
    grad_attended = grad_attended.astype(jnp.bfloat16)
    key_heads = heads_last(window_kv[..., :features])
    value_heads = heads_last(window_kv[..., features:])
    query_heads = heads_last(queries)
    grad_heads = heads_last(grad_attended)
    allowed = (query_line[:, None] == window_line[None, :])[None, None, :, :]
    attention = attention_of(pair_scores(query_heads, key_heads), log_total, allowed)
    grad_prob = jnp.einsum(
        "bhdq,bhdk->bhqk",
        grad_heads,
        value_heads,
        preferred_element_type=jnp.float32,
        precision=highest,
    )
    row_dot = jnp.sum(attention * grad_prob, axis=-1)
    grad_score = (attention * (grad_prob - row_dot[..., None])).astype(jnp.bfloat16)
    grad_query = jnp.einsum(
        "bhqk,bhdk->bhdq",
        grad_score,
        key_heads,
        preferred_element_type=jnp.float32,
        precision=highest,
    )
    grad_query = tokens_last_back(grad_query * HS ** (-0.5), stream.shape).astype(jnp.bfloat16)
    stats_shape = (batches, half_tok, half_tok, time_tok, HEADS)
    total_tokens = jnp.transpose(log_total, (0, 2, 1)).reshape(stats_shape)
    dot_tokens = jnp.transpose(row_dot, (0, 2, 1)).reshape(stats_shape)
    neighbours = (
        extended(queries, (("shot", 1), ("rec", 2)), half_tok),
        extended(grad_attended.astype(jnp.float32), (("shot", 1), ("rec", 2)), half_tok),
    )
    statistics = (
        extended(total_tokens, (("shot", 1), ("rec", 2)), half_tok),
        extended(dot_tokens, (("shot", 1), ("rec", 2)), half_tok),
    )
    window_queries = heads_last(window_region(neighbours[0], shot_at, rec_at))
    window_grads = heads_last(window_region(neighbours[1], shot_at, rec_at).astype(jnp.bfloat16))
    window_total = jnp.transpose(
        window_region(statistics[0], shot_at, rec_at).reshape(batches, -1, HEADS), (0, 2, 1)
    )
    window_dot = jnp.transpose(
        window_region(statistics[1], shot_at, rec_at).reshape(batches, -1, HEADS), (0, 2, 1)
    )
    own_kv = lax.dynamic_slice(
        window_kv,
        (0, half_tok - shot_at, half_tok - rec_at, 0, 0),
        (batches, half_tok, half_tok, time_tok, 2 * features),
    )
    own_keys = heads_last(own_kv[..., :features])
    own_values = heads_last(own_kv[..., features:])
    column_allowed = (window_line[:, None] == query_line[None, :])[None, None, :, :]
    column_attention = attention_of(
        pair_scores(window_queries, own_keys), window_total, column_allowed
    )
    column_grad = jnp.einsum(
        "bhdq,bhdk->bhqk",
        window_grads,
        own_values,
        preferred_element_type=jnp.float32,
        precision=highest,
    )
    column_score = (column_attention * (column_grad - window_dot[..., None])).astype(jnp.bfloat16)
    grad_key = jnp.einsum(
        "bhqk,bhdq->bhdk",
        column_score,
        window_queries,
        preferred_element_type=jnp.float32,
        precision=highest,
    )
    grad_key = tokens_last_back(grad_key * HS ** (-0.5), stream.shape).astype(jnp.bfloat16)
    grad_value = jnp.einsum(
        "bhqk,bhdq->bhdk",
        column_attention.astype(jnp.bfloat16),
        window_grads,
        preferred_element_type=jnp.float32,
    )
    grad_value = tokens_last_back(grad_value, stream.shape).astype(jnp.bfloat16)
    grad_packed = jnp.concatenate([grad_query, grad_key, grad_value], axis=-1)
    grad_normed = lax.dot_general(
        grad_packed, w_layer, contract, preferred_element_type=jnp.float32
    )
    normed_f = stream * inverse
    centred = grad_normed - normed_f * jnp.mean(grad_normed * normed_f, axis=-1, keepdims=True)
    return grad_next + inverse * centred


def local(noisy, misfit, timestep, segment_ids, w_qkv, w_out):
    c_skip, c_out, c_in = precondition(timestep)
    misfit_f = misfit.astype(jnp.float32)
    square_sum = lax.psum(jnp.sum(misfit_f * misfit_f), ("shot", "rec"))
    entries = misfit.size * lax.axis_size("shot") * lax.axis_size("rec")
    misfit_scale = lax.rsqrt(square_sum / entries + norm_eps)
    noisy_f = noisy.astype(jnp.float32)
    start = c_in * noisy_f
    middle, first_saved = block_ahead(start, w_qkv[0], w_out[0], segment_ids, False)
    final, second_saved = block_ahead(middle, w_qkv[1], w_out[1], segment_ids, True)
    denoised = (c_skip * noisy_f + c_out * final).astype(jnp.bfloat16)
    weight = misfit_f * misfit_scale
    grad_middle = block_back(c_out * weight, second_saved, w_qkv[1], w_out[1])
    grad_start = block_back(grad_middle, first_saved, w_qkv[0], w_out[0])
    guidance = (c_skip * weight + c_in * grad_start).astype(jnp.bfloat16)
    return (denoised, guidance)


def solution(mesh):
    placed = (
        P(None, "shot", "rec", None, None),
        P(None, "shot", "rec", None, None),
        P(),
        P(),
        P(),
        P(),
    )
    return jax.shard_map(
        local,
        mesh=mesh,
        in_specs=placed,
        out_specs=(P(None, "shot", "rec", None, None), P(None, "shot", "rec", None, None)),
        check_vma=False,
    )
```

profile of v0, /device:TPU:6, one launch (start us, length us, event | category | flops | bytes accessed | tf_op | source)
XLA Modules:
  0.0 717.1 jit_solution(5488576815788367565)
XLA Ops:
  7.3 13.4 %collective-permute-start.1 = (f32[1,4,4,8,1024]{4,3,2,1,0:T(8,128)S(1)}, f32[1,4,4,8,1024]{4,3,2,1,0:T(8,128)S(1)}, u32[]{:S(2)}, u32[]{:S(2)}) collective-permute-start(f32[1,4,4,8,1024]{4,3,2,1,0:T(8,128)S(1)} %slice.78), channel_id=1, source_target_pairs={{8,0},{16,8},{24,16},{32,24},{40,32},{48,40},{56,48},{64,56},{72,6... | collective-permute-start | bytes 1572872 | tf_op jit(solution)/shard_map/ppermute | solution.py:28
  21.4 93.4 %psum.7 = f32[]{:T(128)} all-reduce(f32[]{:T(128)} %fusion.156), channel_id=1, replica_groups=mesh['shot'=64,'rec'=8] {'shot','rec'}, use_global_device_ids=true, to_apply=%region_7.10 | all-reduce | flops 1 | bytes 8 | tf_op jit(solution)/shard_map/psum | solution.py:249
  117.7 7.6 %collective-permute-start.17 = (bf16[1,4,4,8,512]{4,3,2,1,0:T(8,128)(2,1)S(1)}, bf16[1,4,4,8,512]{4,3,2,1,0:T(8,128)(2,1)}, u32[]{:S(2)}, u32[]{:S(2)}) collective-permute-start(bf16[1,4,4,8,512]{4,3,2,1,0:T(8,128)(2,1)S(1)} %bitcast.328), channel_id=1, source_target_pairs={{8,0},{16,8},{24,16},{32,24},{40,32},{48,40},{56,48},{64,56},{72,6... | collective-permute-start | bytes 393224 | tf_op jit(solution)/shard_map/ppermute | solution.py:28
  130.5 8.1 %collective-permute-start.2 = (f32[1,12,4,8,1024]{4,3,2,1,0:T(8,128)}, f32[1,12,4,8,1024]{4,3,2,1,0:T(8,128)}, u32[]{:S(2)}, u32[]{:S(2)}) collective-permute-start(f32[1,12,4,8,1024]{4,3,2,1,0:T(8,128)} %pad_maximum_fusion.2), channel_id=1, source_target_pairs={{0,1},{1,2},{2,3},{3,4},{4,5},{5,6},{6,7},{7,0},{8,9},{9,10},{10,1... | collective-permute-start | bytes 4718600 | tf_op jit(solution)/shard_map/ppermute | solution.py:27
  145.0 58.2 %collective-permute-done.2 = f32[1,12,4,8,1024]{4,3,2,1,0:T(8,128)} collective-permute-done((f32[1,12,4,8,1024]{4,3,2,1,0:T(8,128)}, f32[1,12,4,8,1024]{4,3,2,1,0:T(8,128)}, u32[]{:S(2)}, u32[]{:S(2)}) %collective-permute-start.2) | collective-permute-done | bytes 1572896 | tf_op jit(solution)/shard_map/ppermute | solution.py:27
  203.2 10.0 %collective-permute-done.3 = f32[1,12,4,8,1024]{4,3,2,1,0:T(8,128)} collective-permute-done((f32[1,12,4,8,1024]{4,3,2,1,0:T(8,128)}, f32[1,12,4,8,1024]{4,3,2,1,0:T(8,128)}, u32[]{:S(2)}, u32[]{:S(2)}) %collective-permute-start.3) | collective-permute-done | bytes 1572896 | tf_op jit(solution)/shard_map/ppermute | solution.py:28
  220.5 2.8 copy.62
  223.3 4.0 select_reduce_fusion.3
  233.2 2.8 copy.60
  236.1 5.0 fusion.68
  248.1 8.1 %collective-permute-start.5 = (f32[1,4,4,8,1024]{4,3,2,1,0:T(8,128)S(1)}, f32[1,4,4,8,1024]{4,3,2,1,0:T(8,128)S(1)}, u32[]{:S(2)}, u32[]{:S(2)}) collective-permute-start(f32[1,4,4,8,1024]{4,3,2,1,0:T(8,128)S(1)} %slice.80), channel_id=1, source_target_pairs={{8,0},{16,8},{24,16},{32,24},{40,32},{48,40},{56,48},{64,56},{72,6... | collective-permute-start | bytes 1572872 | tf_op jit(solution)/shard_map/ppermute | solution.py:28
  266.7 3.9 collective-permute-start.19
  274.0 7.9 %collective-permute-start.26 = (f32[1,12,4,8,512]{4,3,2,1,0:T(8,128)}, f32[1,12,4,8,512]{4,3,2,1,0:T(8,128)}, u32[]{:S(2)}, u32[]{:S(2)}) collective-permute-start(f32[1,12,4,8,512]{4,3,2,1,0:T(8,128)} %pad_maximum_fusion.6), channel_id=1, source_target_pairs={{0,1},{1,2},{2,3},{3,4},{4,5},{5,6},{6,7},{7,0},{8,9},{9,10},{10,1... | collective-permute-start | bytes 2359304 | tf_op jit(solution)/shard_map/ppermute | solution.py:27
  288.8 9.9 %collective-permute-start.6 = (f32[1,12,4,8,1024]{4,3,2,1,0:T(8,128)}, f32[1,12,4,8,1024]{4,3,2,1,0:T(8,128)}, u32[]{:S(2)}, u32[]{:S(2)}) collective-permute-start(f32[1,12,4,8,1024]{4,3,2,1,0:T(8,128)} %pad_maximum_fusion.3), channel_id=1, source_target_pairs={{0,1},{1,2},{2,3},{3,4},{4,5},{5,6},{6,7},{7,0},{8,9},{9,10},{10,1... | collective-permute-start | bytes 4718600 | tf_op jit(solution)/shard_map/ppermute | solution.py:27
  302.7 17.6 %collective-permute-done.8 = f32[1,4,4,8,512]{4,3,2,1,0:T(8,128)} collective-permute-done((f32[1,4,4,8,512]{4,3,2,1,0:T(8,128)}, f32[1,4,4,8,512]{4,3,2,1,0:T(8,128)}, u32[]{:S(2)}, u32[]{:S(2)}) %collective-permute-start.8) | collective-permute-done | bytes 262176 | tf_op jit(solution)/shard_map/ppermute | solution.py:27
  330.9 53.8 %collective-permute-done.9 = f32[1,4,4,8,512]{4,3,2,1,0:T(8,128)} collective-permute-done((f32[1,4,4,8,512]{4,3,2,1,0:T(8,128)}, f32[1,4,4,8,512]{4,3,2,1,0:T(8,128)}, u32[]{:S(2)}, u32[]{:S(2)}) %collective-permute-start.9) | collective-permute-done | bytes 262176 | tf_op jit(solution)/shard_map/ppermute | solution.py:28
  388.7 8.0 %collective-permute-start.29 = (f32[1,4,4,8,16]{4,3,2,1,0:T(8,128)S(1)}, f32[1,4,4,8,16]{4,3,2,1,0:T(8,128)S(1)}, u32[]{:S(2)}, u32[]{:S(2)}) collective-permute-start(f32[1,4,4,8,16]{4,3,2,1,0:T(8,128)S(1)} %bitcast.340), channel_id=1, source_target_pairs={{8,0},{16,8},{24,16},{32,24},{40,32},{48,40},{56,48},{64,56},{72,6... | collective-permute-start | bytes 24584 | tf_op jit(solution)/shard_map/ppermute | solution.py:28
  396.7 8.3 %collective-permute-start.10 = (f32[1,12,4,8,512]{4,3,2,1,0:T(8,128)}, f32[1,12,4,8,512]{4,3,2,1,0:T(8,128)}, u32[]{:S(2)}, u32[]{:S(2)}) collective-permute-start(f32[1,12,4,8,512]{4,3,2,1,0:T(8,128)} %pad_maximum_fusion.4), channel_id=1, source_target_pairs={{0,1},{1,2},{2,3},{3,4},{4,5},{5,6},{6,7},{7,0},{8,9},{9,10},{10,1... | collective-permute-start | bytes 2359304 | tf_op jit(solution)/shard_map/ppermute | solution.py:27
  411.3 2.8 copy.82
  414.8 10.0 %collective-permute-start.30 = (f32[1,12,4,8,16]{4,3,2,1,0:T(8,128)}, f32[1,12,4,8,16]{4,3,2,1,0:T(8,128)}, u32[]{:S(2)}, u32[]{:S(2)}) collective-permute-start(f32[1,12,4,8,16]{4,3,2,1,0:T(8,128)} %pad_maximum_fusion.10), channel_id=1, source_target_pairs={{0,1},{1,2},{2,3},{3,4},{4,5},{5,6},{6,7},{7,0},{8,9},{9,10},{10,1... | collective-permute-start | bytes 73736 | tf_op jit(solution)/shard_map/ppermute | solution.py:27
  429.0 12.6 %collective-permute-done.30 = f32[1,12,4,8,16]{4,3,2,1,0:T(8,128)} collective-permute-done((f32[1,12,4,8,16]{4,3,2,1,0:T(8,128)}, f32[1,12,4,8,16]{4,3,2,1,0:T(8,128)}, u32[]{:S(2)}, u32[]{:S(2)}) %collective-permute-start.30) | collective-permute-done | bytes 24608 | tf_op jit(solution)/shard_map/ppermute | solution.py:27
  443.7 9.2 %fusion.100 = f32[16,512,128]{2,1,0:T(8,128)} fusion(f32[1,512,16,32]{1,3,2,0:T(8,128)S(1)} %copy.82, f32[1,128,16,32]{1,3,2,0:T(8,128)} %copy.83), kind=kOutput, calls=%fused_computation.125 | convolution fusion | flops 402653184 | bytes 5505024 | tf_op jit(solution)/shard_map/bhdq,bhdk->bhqk/dot_general | solution.py:93
  462.9 2.8 copy.70
  472.2 3.8 reshape.740
  476.0 3.8 copy.66
  479.8 5.3 select_reduce_fusion.1
  488.3 3.8 reshape.736
  492.0 3.6 copy.64
  495.7 7.6 %multiply_reduce_fusion.1 = (f32[16,128]{1,0:T(8,128)S(1)}, f32[16,128,512]{2,1,0:T(8,128)}) fusion(f32[16,128,512]{2,1,0:T(8,128)} %copy-done.3, f32[16,128]{1,0:T(8,128)S(1)} %log_add_fusion, pred[128,512]{1,0:T(8,128)(4,1)S(1)} %copy-done.19, f32[1,512,16,32]{1,3,2,0:T(8,128)} %copy.64, bf16[16,32,128]{1,0,2:T(8,128)(2,1)} %bitcast.325), kind=kOutput, calls=%fused_computation.12 | convolution fusion | flops 407894016 | bytes 9650176 | tf_op jit(solution)/shard_map/bhdq,bhdk->bhqk/dot_general | solution.py:167
  505.9 7.6 %collective-permute-start.21 = (f32[1,4,4,8,16]{4,3,2,1,0:T(8,128)}, f32[1,4,4,8,16]{4,3,2,1,0:T(8,128)}, u32[]{:S(2)}, u32[]{:S(2)}) collective-permute-start(f32[1,4,4,8,16]{4,3,2,1,0:T(8,128)} %bitcast.65), channel_id=1, source_target_pairs={{8,0},{16,8},{24,16},{32,24},{40,32},{48,40},{56,48},{64,56},{72,6... | collective-permute-start | bytes 24584 | tf_op jit(solution)/shard_map/ppermute | solution.py:28
  516.5 7.8 %collective-permute-start.13 = (f32[1,4,4,8,16]{4,3,2,1,0:T(8,128)}, f32[1,4,4,8,16]{4,3,2,1,0:T(8,128)}, u32[]{:S(2)}, u32[]{:S(2)}) collective-permute-start(f32[1,4,4,8,16]{4,3,2,1,0:T(8,128)} %bitcast.53), channel_id=1, source_target_pairs={{8,0},{16,8},{24,16},{32,24},{40,32},{48,40},{56,48},{64,56},{72,6... | collective-permute-start | bytes 24584 | tf_op jit(solution)/shard_map/ppermute | solution.py:28
  524.3 5.6 fusion.65
  529.9 5.8 fusion.80
  542.0 9.2 %fusion.109 = f32[16,512,128]{2,1,0:T(8,128)} fusion(f32[1,512,16,32]{1,3,2,0:T(8,128)S(1)} %copy.70, f32[1,128,16,32]{1,3,2,0:T(8,128)} %copy.71), kind=kOutput, calls=%fused_computation.134 | convolution fusion | flops 402653184 | bytes 5505024 | tf_op jit(solution)/shard_map/bhdq,bhdk->bhqk/dot_general | solution.py:93
  564.2 10.5 %collective-permute-start.22 = (f32[1,12,4,8,16]{4,3,2,1,0:T(8,128)S(1)}, f32[1,12,4,8,16]{4,3,2,1,0:T(8,128)S(1)}, u32[]{:S(2)}, u32[]{:S(2)}) collective-permute-start(f32[1,12,4,8,16]{4,3,2,1,0:T(8,128)S(1)} %pad_maximum_fusion.9), channel_id=1, source_target_pairs={{0,1},{1,2},{2,3},{3,4},{4,5},{5,6},{6,7},{7,0},{8,9},{9,10},{10,1... | collective-permute-start | bytes 73736 | tf_op jit(solution)/shard_map/ppermute | solution.py:27
  578.3 9.9 %collective-permute-start.14 = (f32[1,12,4,8,16]{4,3,2,1,0:T(8,128)}, f32[1,12,4,8,16]{4,3,2,1,0:T(8,128)}, u32[]{:S(2)}, u32[]{:S(2)}) collective-permute-start(f32[1,12,4,8,16]{4,3,2,1,0:T(8,128)} %pad_maximum_fusion.8), channel_id=1, source_target_pairs={{0,1},{1,2},{2,3},{3,4},{4,5},{5,6},{6,7},{7,0},{8,9},{9,10},{10,1... | collective-permute-start | bytes 73736 | tf_op jit(solution)/shard_map/ppermute | solution.py:27
  593.7 10.4 %collective-permute-done.15 = f32[1,12,4,8,16]{4,3,2,1,0:T(8,128)} collective-permute-done((f32[1,12,4,8,16]{4,3,2,1,0:T(8,128)}, f32[1,12,4,8,16]{4,3,2,1,0:T(8,128)}, u32[]{:S(2)}, u32[]{:S(2)}) %collective-permute-start.15) | collective-permute-done | bytes 24608 | tf_op jit(solution)/shard_map/ppermute | solution.py:28
  606.0 4.1 fusion.74
  610.1 4.7 multiply_convert_fusion.2
  632.0 7.8 %multiply_reduce_fusion = (f32[16,128]{1,0:T(8,128)}, f32[16,128,512]{2,1,0:T(8,128)}) fusion(f32[16,128,512]{2,1,0:T(8,128)} %copy-done.2, f32[16,128]{1,0:T(8,128)S(1)} %log_add_fusion.1, pred[128,512]{1,0:T(8,128)(4,1)} %copy-done.18, f32[1,512,16,32]{1,3,2,0:T(8,128)S(1)} %copy-done.10, bf16[16,32,128]{1,0,2:T(8,128)(2,1)} %bitcast.326), kind=kOutput, calls=%fused_computation.8 | convolution fusion | flops 407894016 | bytes 9650176 | tf_op jit(solution)/shard_map/bhdq,bhdk->bhqk/dot_general | solution.py:167
  642.5 7.5 %collective-permute-start.37 = (f32[1,4,4,8,16]{4,3,2,1,0:T(8,128)S(1)}, f32[1,4,4,8,16]{4,3,2,1,0:T(8,128)S(1)}, u32[]{:S(2)}, u32[]{:S(2)}) collective-permute-start(f32[1,4,4,8,16]{4,3,2,1,0:T(8,128)S(1)} %bitcast.344), channel_id=1, source_target_pairs={{8,0},{16,8},{24,16},{32,24},{40,32},{48,40},{56,48},{64,56},{72,6... | collective-permute-start | bytes 24584 | tf_op jit(solution)/shard_map/ppermute | solution.py:28
  651.9 7.5 %collective-permute-start.33 = (bf16[1,4,4,8,512]{4,3,2,1,0:T(8,128)(2,1)}, bf16[1,4,4,8,512]{4,3,2,1,0:T(8,128)(2,1)S(1)}, u32[]{:S(2)}, u32[]{:S(2)}) collective-permute-start(bf16[1,4,4,8,512]{4,3,2,1,0:T(8,128)(2,1)} %bitcast.332), channel_id=1, source_target_pairs={{8,0},{16,8},{24,16},{32,24},{40,32},{48,40},{56,48},{64,56},{72,6... | collective-permute-start | bytes 393224 | tf_op jit(solution)/shard_map/ppermute | solution.py:28
  663.5 3.9 collective-permute-start.39
  669.1 7.9 %collective-permute-start.34 = (bf16[1,12,4,8,512]{4,3,2,1,0:T(8,128)(2,1)}, bf16[1,12,4,8,512]{4,3,2,1,0:T(8,128)(2,1)}, u32[]{:S(2)}, u32[]{:S(2)}) collective-permute-start(bf16[1,12,4,8,512]{4,3,2,1,0:T(8,128)(2,1)} %pad_maximum_fusion.7), channel_id=1, source_target_pairs={{0,1},{1,2},{2,3},{3,4},{4,5},{5,6},{6,7},{7,0},{8,9},{9,10},{10,1... | collective-permute-start | bytes 1179656 | tf_op jit(solution)/shard_map/ppermute | solution.py:27
  679.2 6.3 fusion.79
  688.4 7.9 %collective-permute-done.35 = bf16[1,12,4,8,512]{4,3,2,1,0:T(8,128)(2,1)} collective-permute-done((bf16[1,12,4,8,512]{4,3,2,1,0:T(8,128)(2,1)}, bf16[1,12,4,8,512]{4,3,2,1,0:T(8,128)(2,1)}, u32[]{:S(2)}, u32[]{:S(2)}) %collective-permute-start.35) | collective-permute-done | bytes 393248 | tf_op jit(solution)/shard_map/ppermute | solution.py:28
  702.7 3.3 fusion.71
  706.1 4.7 multiply_convert_fusion
  (285 shorter events, 192.7 us)
Async XLA Ops:
  0.6 127.9 %copy-start = (s32[256]{0:T(256)S(1)}, s32[256]{0:T(256)}, u32[]{:S(2)}) copy-start(s32[256]{0:T(256)} %param.13) | copy-start | bytes 3076
  0.7 114.8 %copy-start.23 = (bf16[2,512,512]{2,1,0:T(8,128)(2,1)S(1)}, bf16[2,512,512]{2,1,0:T(8,128)(2,1)}, u32[]{:S(2)}) copy-start(bf16[2,512,512]{2,1,0:T(8,128)(2,1)} %param.15) | copy-start | bytes 3145732
  5.4 123.8 %collective-permute-start = (f32[1,4,4,8,1024]{4,3,2,1,0:T(8,128)S(1)}, f32[1,4,4,8,1024]{4,3,2,1,0:T(8,128)S(1)}, u32[]{:S(2)}, u32[]{:S(2)}) collective-permute-start(f32[1,4,4,8,1024]{4,3,2,1,0:T(8,128)S(1)} %slice.78), channel_id=1, source_target_pairs={{0,8},{8,16},{16,24},{24,32},{32,40},{40,48},{48,56},{56,64},{64,7... | collective-permute-start | bytes 1572872 | tf_op jit(solution)/shard_map/ppermute | solution.py:27
  7.3 121.9 %collective-permute-start.1 = (f32[1,4,4,8,1024]{4,3,2,1,0:T(8,128)S(1)}, f32[1,4,4,8,1024]{4,3,2,1,0:T(8,128)S(1)}, u32[]{:S(2)}, u32[]{:S(2)}) collective-permute-start(f32[1,4,4,8,1024]{4,3,2,1,0:T(8,128)S(1)} %slice.78), channel_id=1, source_target_pairs={{8,0},{16,8},{24,16},{32,24},{40,32},{48,40},{56,48},{64,56},{72,6... | collective-permute-start | bytes 1572872 | tf_op jit(solution)/shard_map/ppermute | solution.py:28
  115.8 145.9 %collective-permute-start.16 = (bf16[1,4,4,8,512]{4,3,2,1,0:T(8,128)(2,1)S(1)}, bf16[1,4,4,8,512]{4,3,2,1,0:T(8,128)(2,1)S(1)}, u32[]{:S(2)}, u32[]{:S(2)}) collective-permute-start(bf16[1,4,4,8,512]{4,3,2,1,0:T(8,128)(2,1)S(1)} %bitcast.327), channel_id=1, source_target_pairs={{0,8},{8,16},{16,24},{24,32},{32,40},{40,48},{48,56},{56,64},{64,7... | collective-permute-start | bytes 393224 | tf_op jit(solution)/shard_map/ppermute | solution.py:27
  117.7 146.0 %collective-permute-start.17 = (bf16[1,4,4,8,512]{4,3,2,1,0:T(8,128)(2,1)S(1)}, bf16[1,4,4,8,512]{4,3,2,1,0:T(8,128)(2,1)}, u32[]{:S(2)}, u32[]{:S(2)}) collective-permute-start(bf16[1,4,4,8,512]{4,3,2,1,0:T(8,128)(2,1)S(1)} %bitcast.328), channel_id=1, source_target_pairs={{8,0},{16,8},{24,16},{32,24},{40,32},{48,40},{56,48},{64,56},{72,6... | collective-permute-start | bytes 393224 | tf_op jit(solution)/shard_map/ppermute | solution.py:28
  126.3 140.4 %collective-permute-start.24 = (f32[1,4,4,8,512]{4,3,2,1,0:T(8,128)S(1)}, f32[1,4,4,8,512]{4,3,2,1,0:T(8,128)}, u32[]{:S(2)}, u32[]{:S(2)}) collective-permute-start(f32[1,4,4,8,512]{4,3,2,1,0:T(8,128)S(1)} %slice.79), channel_id=1, source_target_pairs={{0,8},{8,16},{16,24},{24,32},{32,40},{40,48},{48,56},{56,64},{64,7... | collective-permute-start | bytes 786440 | tf_op jit(solution)/shard_map/ppermute | solution.py:27
  130.5 72.7 %collective-permute-start.2 = (f32[1,12,4,8,1024]{4,3,2,1,0:T(8,128)}, f32[1,12,4,8,1024]{4,3,2,1,0:T(8,128)}, u32[]{:S(2)}, u32[]{:S(2)}) collective-permute-start(f32[1,12,4,8,1024]{4,3,2,1,0:T(8,128)} %pad_maximum_fusion.2), channel_id=1, source_target_pairs={{0,1},{1,2},{2,3},{3,4},{4,5},{5,6},{6,7},{7,0},{8,9},{9,10},{10,1... | collective-permute-start | bytes 4718600 | tf_op jit(solution)/shard_map/ppermute | solution.py:27
  138.7 74.5 %collective-permute-start.3 = (f32[1,12,4,8,1024]{4,3,2,1,0:T(8,128)}, f32[1,12,4,8,1024]{4,3,2,1,0:T(8,128)}, u32[]{:S(2)}, u32[]{:S(2)}) collective-permute-start(f32[1,12,4,8,1024]{4,3,2,1,0:T(8,128)} %pad_maximum_fusion.2), channel_id=1, source_target_pairs={{1,0},{2,1},{3,2},{4,3},{5,4},{6,5},{7,6},{0,7},{9,8},{10,9},{11,1... | collective-permute-start | bytes 4718600 | tf_op jit(solution)/shard_map/ppermute | solution.py:28
  142.4 73.1 %copy-start.52 = (s32[128]{0:T(128)}, s32[128]{0:T(128)S(1)}, u32[]{:S(2)}) copy-start(s32[128]{0:T(128)S(1)} %eq.99) | copy-start | bytes 1540
  145.0 91.1 %copy-start.18 = (pred[128,512]{1,0:T(8,128)(4,1)}, pred[128,512]{1,0:T(8,128)(4,1)S(1)}, u32[]{:S(2)}) copy-start(pred[128,512]{1,0:T(8,128)(4,1)S(1)} %broadcast_compare_fusion.3) | copy-start | bytes 196612
  243.4 45.4 %copy-start.13 = (f32[1,4,4,8,512]{4,3,2,1,0:T(8,128)}, f32[1,4,4,8,512]{4,3,2,1,0:T(8,128)S(1)}, u32[]{:S(2)}) copy-start(f32[1,4,4,8,512]{4,3,2,1,0:T(8,128)S(1)} %get-tuple-element.17) | copy-start | bytes 786436
  246.2 77.3 %copy-start.8 = (f32[1,4,4,8,1024]{4,3,2,1,0:T(8,128)}, f32[1,4,4,8,1024]{4,3,2,1,0:T(8,128)S(1)}, u32[]{:S(2)}) copy-start(f32[1,4,4,8,1024]{4,3,2,1,0:T(8,128)S(1)} %slice.80) | copy-start | bytes 1572868
  246.2 37.4 %collective-permute-start.4 = (f32[1,4,4,8,1024]{4,3,2,1,0:T(8,128)S(1)}, f32[1,4,4,8,1024]{4,3,2,1,0:T(8,128)S(1)}, u32[]{:S(2)}, u32[]{:S(2)}) collective-permute-start(f32[1,4,4,8,1024]{4,3,2,1,0:T(8,128)S(1)} %slice.80), channel_id=1, source_target_pairs={{0,8},{8,16},{16,24},{24,32},{32,40},{40,48},{48,56},{56,64},{64,7... | collective-permute-start | bytes 1572872 | tf_op jit(solution)/shard_map/ppermute | solution.py:27
  248.1 37.4 %collective-permute-start.5 = (f32[1,4,4,8,1024]{4,3,2,1,0:T(8,128)S(1)}, f32[1,4,4,8,1024]{4,3,2,1,0:T(8,128)S(1)}, u32[]{:S(2)}, u32[]{:S(2)}) collective-permute-start(f32[1,4,4,8,1024]{4,3,2,1,0:T(8,128)S(1)} %slice.80), channel_id=1, source_target_pairs={{8,0},{16,8},{24,16},{32,24},{40,32},{48,40},{56,48},{64,56},{72,6... | collective-permute-start | bytes 1572872 | tf_op jit(solution)/shard_map/ppermute | solution.py:28
  261.7 10.3 %collective-permute-start.25 = (f32[1,4,4,8,512]{4,3,2,1,0:T(8,128)S(1)}, f32[1,4,4,8,512]{4,3,2,1,0:T(8,128)S(1)}, u32[]{:S(2)}, u32[]{:S(2)}) collective-permute-start(f32[1,4,4,8,512]{4,3,2,1,0:T(8,128)S(1)} %slice.79), channel_id=1, source_target_pairs={{8,0},{16,8},{24,16},{32,24},{40,32},{48,40},{56,48},{64,56},{72,6... | collective-permute-start | bytes 786440 | tf_op jit(solution)/shard_map/ppermute | solution.py:28
  264.7 24.1 %collective-permute-start.18 = (bf16[1,12,4,8,512]{4,3,2,1,0:T(8,128)(2,1)S(1)}, bf16[1,12,4,8,512]{4,3,2,1,0:T(8,128)(2,1)S(1)}, u32[]{:S(2)}, u32[]{:S(2)}) collective-permute-start(bf16[1,12,4,8,512]{4,3,2,1,0:T(8,128)(2,1)S(1)} %pad_maximum_fusion.5), channel_id=1, source_target_pairs={{0,1},{1,2},{2,3},{3,4},{4,5},{5,6},{6,7},{7,0},{8,9},{9,10},{10,1... | collective-permute-start | bytes 1179656 | tf_op jit(solution)/shard_map/ppermute | solution.py:27
  266.7 32.1 %collective-permute-start.19 = (bf16[1,12,4,8,512]{4,3,2,1,0:T(8,128)(2,1)S(1)}, bf16[1,12,4,8,512]{4,3,2,1,0:T(8,128)(2,1)S(1)}, u32[]{:S(2)}, u32[]{:S(2)}) collective-permute-start(bf16[1,12,4,8,512]{4,3,2,1,0:T(8,128)(2,1)S(1)} %pad_maximum_fusion.5), channel_id=1, source_target_pairs={{1,0},{2,1},{3,2},{4,3},{5,4},{6,5},{7,6},{0,7},{9,8},{10,9},{11,1... | collective-permute-start | bytes 1179656 | tf_op jit(solution)/shard_map/ppermute | solution.py:28
  274.0 114.6 %collective-permute-start.26 = (f32[1,12,4,8,512]{4,3,2,1,0:T(8,128)}, f32[1,12,4,8,512]{4,3,2,1,0:T(8,128)}, u32[]{:S(2)}, u32[]{:S(2)}) collective-permute-start(f32[1,12,4,8,512]{4,3,2,1,0:T(8,128)} %pad_maximum_fusion.6), channel_id=1, source_target_pairs={{0,1},{1,2},{2,3},{3,4},{4,5},{5,6},{6,7},{7,0},{8,9},{9,10},{10,1... | collective-permute-start | bytes 2359304 | tf_op jit(solution)/shard_map/ppermute | solution.py:27
  283.6 39.9 %copy-start.15 = (f32[1,4,4,8,1024]{4,3,2,1,0:T(8,128)}, f32[1,4,4,8,1024]{4,3,2,1,0:T(8,128)S(1)}, u32[]{:S(2)}) copy-start(f32[1,4,4,8,1024]{4,3,2,1,0:T(8,128)S(1)} %collective-permute-done.4) | copy-start | bytes 1572868
  283.6 113.0 %collective-permute-start.27 = (f32[1,12,4,8,512]{4,3,2,1,0:T(8,128)}, f32[1,12,4,8,512]{4,3,2,1,0:T(8,128)}, u32[]{:S(2)}, u32[]{:S(2)}) collective-permute-start(f32[1,12,4,8,512]{4,3,2,1,0:T(8,128)} %pad_maximum_fusion.6), channel_id=1, source_target_pairs={{1,0},{2,1},{3,2},{4,3},{5,4},{6,5},{7,6},{0,7},{9,8},{10,9},{11,1... | collective-permute-start | bytes 2359304 | tf_op jit(solution)/shard_map/ppermute | solution.py:28
  285.6 34.7 %collective-permute-start.8 = (f32[1,4,4,8,512]{4,3,2,1,0:T(8,128)}, f32[1,4,4,8,512]{4,3,2,1,0:T(8,128)}, u32[]{:S(2)}, u32[]{:S(2)}) collective-permute-start(f32[1,4,4,8,512]{4,3,2,1,0:T(8,128)} %slice.81), channel_id=1, source_target_pairs={{0,8},{8,16},{16,24},{24,32},{32,40},{40,48},{48,56},{56,64},{64,7... | collective-permute-start | bytes 786440 | tf_op jit(solution)/shard_map/ppermute | solution.py:27
  288.8 176.9 %collective-permute-start.6 = (f32[1,12,4,8,1024]{4,3,2,1,0:T(8,128)}, f32[1,12,4,8,1024]{4,3,2,1,0:T(8,128)}, u32[]{:S(2)}, u32[]{:S(2)}) collective-permute-start(f32[1,12,4,8,1024]{4,3,2,1,0:T(8,128)} %pad_maximum_fusion.3), channel_id=1, source_target_pairs={{0,1},{1,2},{2,3},{3,4},{4,5},{5,6},{6,7},{7,0},{8,9},{9,10},{10,1... | collective-permute-start | bytes 4718600 | tf_op jit(solution)/shard_map/ppermute | solution.py:27
  298.8 167.0 %collective-permute-start.7 = (f32[1,12,4,8,1024]{4,3,2,1,0:T(8,128)}, f32[1,12,4,8,1024]{4,3,2,1,0:T(8,128)}, u32[]{:S(2)}, u32[]{:S(2)}) collective-permute-start(f32[1,12,4,8,1024]{4,3,2,1,0:T(8,128)} %pad_maximum_fusion.3), channel_id=1, source_target_pairs={{1,0},{2,1},{3,2},{4,3},{5,4},{6,5},{7,6},{0,7},{9,8},{10,9},{11,1... | collective-permute-start | bytes 4718600 | tf_op jit(solution)/shard_map/ppermute | solution.py:28
  320.3 64.5 %collective-permute-start.9 = (f32[1,4,4,8,512]{4,3,2,1,0:T(8,128)}, f32[1,4,4,8,512]{4,3,2,1,0:T(8,128)}, u32[]{:S(2)}, u32[]{:S(2)}) collective-permute-start(f32[1,4,4,8,512]{4,3,2,1,0:T(8,128)} %slice.81), channel_id=1, source_target_pairs={{8,0},{16,8},{24,16},{32,24},{40,32},{48,40},{56,48},{64,56},{72,6... | collective-permute-start | bytes 786440 | tf_op jit(solution)/shard_map/ppermute | solution.py:28
  330.9 83.2 %copy-start.27 = (f32[1,128,16]{2,1,0:T(8,128)}, f32[1,128,16]{2,1,0:T(8,128)S(1)}, u32[]{:S(2)}) copy-start(f32[1,128,16]{2,1,0:T(8,128)S(1)} %copy.84) | copy-start | bytes 24580
  384.7 20.3 %collective-permute-start.28 = (f32[1,4,4,8,16]{4,3,2,1,0:T(8,128)S(1)}, f32[1,4,4,8,16]{4,3,2,1,0:T(8,128)S(1)}, u32[]{:S(2)}, u32[]{:S(2)}) collective-permute-start(f32[1,4,4,8,16]{4,3,2,1,0:T(8,128)S(1)} %bitcast.339), channel_id=1, source_target_pairs={{0,8},{8,16},{16,24},{24,32},{32,40},{40,48},{48,56},{56,64},{64,7... | collective-permute-start | bytes 24584 | tf_op jit(solution)/shard_map/ppermute | solution.py:27
  388.7 25.4 %collective-permute-start.29 = (f32[1,4,4,8,16]{4,3,2,1,0:T(8,128)S(1)}, f32[1,4,4,8,16]{4,3,2,1,0:T(8,128)S(1)}, u32[]{:S(2)}, u32[]{:S(2)}) collective-permute-start(f32[1,4,4,8,16]{4,3,2,1,0:T(8,128)S(1)} %bitcast.340), channel_id=1, source_target_pairs={{8,0},{16,8},{24,16},{32,24},{40,32},{48,40},{56,48},{64,56},{72,6... | collective-permute-start | bytes 24584 | tf_op jit(solution)/shard_map/ppermute | solution.py:28
  396.7 61.8 %collective-permute-start.10 = (f32[1,12,4,8,512]{4,3,2,1,0:T(8,128)}, f32[1,12,4,8,512]{4,3,2,1,0:T(8,128)}, u32[]{:S(2)}, u32[]{:S(2)}) collective-permute-start(f32[1,12,4,8,512]{4,3,2,1,0:T(8,128)} %pad_maximum_fusion.4), channel_id=1, source_target_pairs={{0,1},{1,2},{2,3},{3,4},{4,5},{5,6},{6,7},{7,0},{8,9},{9,10},{10,1... | collective-permute-start | bytes 2359304 | tf_op jit(solution)/shard_map/ppermute | solution.py:27
  405.0 53.5 %collective-permute-start.11 = (f32[1,12,4,8,512]{4,3,2,1,0:T(8,128)}, f32[1,12,4,8,512]{4,3,2,1,0:T(8,128)}, u32[]{:S(2)}, u32[]{:S(2)}) collective-permute-start(f32[1,12,4,8,512]{4,3,2,1,0:T(8,128)} %pad_maximum_fusion.4), channel_id=1, source_target_pairs={{1,0},{2,1},{3,2},{4,3},{5,4},{6,5},{7,6},{0,7},{9,8},{10,9},{11,1... | collective-permute-start | bytes 2359304 | tf_op jit(solution)/shard_map/ppermute | solution.py:28
  414.8 26.8 %collective-permute-start.30 = (f32[1,12,4,8,16]{4,3,2,1,0:T(8,128)}, f32[1,12,4,8,16]{4,3,2,1,0:T(8,128)}, u32[]{:S(2)}, u32[]{:S(2)}) collective-permute-start(f32[1,12,4,8,16]{4,3,2,1,0:T(8,128)} %pad_maximum_fusion.10), channel_id=1, source_target_pairs={{0,1},{1,2},{2,3},{3,4},{4,5},{5,6},{6,7},{7,0},{8,9},{9,10},{10,1... | collective-permute-start | bytes 73736 | tf_op jit(solution)/shard_map/ppermute | solution.py:27
  441.6 15.1 %collective-permute-start.31 = (f32[1,12,4,8,16]{4,3,2,1,0:T(8,128)}, f32[1,12,4,8,16]{4,3,2,1,0:T(8,128)}, u32[]{:S(2)}, u32[]{:S(2)}) collective-permute-start(f32[1,12,4,8,16]{4,3,2,1,0:T(8,128)} %pad_maximum_fusion.10), channel_id=1, source_target_pairs={{1,0},{2,1},{3,2},{4,3},{5,4},{6,5},{7,6},{0,7},{9,8},{10,9},{11,1... | collective-permute-start | bytes 73736 | tf_op jit(solution)/shard_map/ppermute | solution.py:28
  503.9 59.3 %collective-permute-start.20 = (f32[1,4,4,8,16]{4,3,2,1,0:T(8,128)}, f32[1,4,4,8,16]{4,3,2,1,0:T(8,128)}, u32[]{:S(2)}, u32[]{:S(2)}) collective-permute-start(f32[1,4,4,8,16]{4,3,2,1,0:T(8,128)} %bitcast.65), channel_id=1, source_target_pairs={{0,8},{8,16},{16,24},{24,32},{32,40},{40,48},{48,56},{56,64},{64,7... | collective-permute-start | bytes 24584 | tf_op jit(solution)/shard_map/ppermute | solution.py:27
  505.9 57.4 %collective-permute-start.21 = (f32[1,4,4,8,16]{4,3,2,1,0:T(8,128)}, f32[1,4,4,8,16]{4,3,2,1,0:T(8,128)}, u32[]{:S(2)}, u32[]{:S(2)}) collective-permute-start(f32[1,4,4,8,16]{4,3,2,1,0:T(8,128)} %bitcast.65), channel_id=1, source_target_pairs={{8,0},{16,8},{24,16},{32,24},{40,32},{48,40},{56,48},{64,56},{72,6... | collective-permute-start | bytes 24584 | tf_op jit(solution)/shard_map/ppermute | solution.py:28
  514.1 62.5 %collective-permute-start.12 = (f32[1,4,4,8,16]{4,3,2,1,0:T(8,128)}, f32[1,4,4,8,16]{4,3,2,1,0:T(8,128)}, u32[]{:S(2)}, u32[]{:S(2)}) collective-permute-start(f32[1,4,4,8,16]{4,3,2,1,0:T(8,128)} %bitcast.53), channel_id=1, source_target_pairs={{0,8},{8,16},{16,24},{24,32},{32,40},{40,48},{48,56},{56,64},{64,7... | collective-permute-start | bytes 24584 | tf_op jit(solution)/shard_map/ppermute | solution.py:27
  516.5 60.2 %collective-permute-start.13 = (f32[1,4,4,8,16]{4,3,2,1,0:T(8,128)}, f32[1,4,4,8,16]{4,3,2,1,0:T(8,128)}, u32[]{:S(2)}, u32[]{:S(2)}) collective-permute-start(f32[1,4,4,8,16]{4,3,2,1,0:T(8,128)} %bitcast.53), channel_id=1, source_target_pairs={{8,0},{16,8},{24,16},{32,24},{40,32},{48,40},{56,48},{64,56},{72,6... | collective-permute-start | bytes 24584 | tf_op jit(solution)/shard_map/ppermute | solution.py:28
  564.2 26.1 %collective-permute-start.22 = (f32[1,12,4,8,16]{4,3,2,1,0:T(8,128)S(1)}, f32[1,12,4,8,16]{4,3,2,1,0:T(8,128)S(1)}, u32[]{:S(2)}, u32[]{:S(2)}) collective-permute-start(f32[1,12,4,8,16]{4,3,2,1,0:T(8,128)S(1)} %pad_maximum_fusion.9), channel_id=1, source_target_pairs={{0,1},{1,2},{2,3},{3,4},{4,5},{5,6},{6,7},{7,0},{8,9},{9,10},{10,1... | collective-permute-start | bytes 73736 | tf_op jit(solution)/shard_map/ppermute | solution.py:27
  574.7 15.6 %collective-permute-start.23 = (f32[1,12,4,8,16]{4,3,2,1,0:T(8,128)S(1)}, f32[1,12,4,8,16]{4,3,2,1,0:T(8,128)S(1)}, u32[]{:S(2)}, u32[]{:S(2)}) collective-permute-start(f32[1,12,4,8,16]{4,3,2,1,0:T(8,128)S(1)} %pad_maximum_fusion.9), channel_id=1, source_target_pairs={{1,0},{2,1},{3,2},{4,3},{5,4},{6,5},{7,6},{0,7},{9,8},{10,9},{11,1... | collective-permute-start | bytes 73736 | tf_op jit(solution)/shard_map/ppermute | solution.py:28
  578.3 15.4 %collective-permute-start.14 = (f32[1,12,4,8,16]{4,3,2,1,0:T(8,128)}, f32[1,12,4,8,16]{4,3,2,1,0:T(8,128)}, u32[]{:S(2)}, u32[]{:S(2)}) collective-permute-start(f32[1,12,4,8,16]{4,3,2,1,0:T(8,128)} %pad_maximum_fusion.8), channel_id=1, source_target_pairs={{0,1},{1,2},{2,3},{3,4},{4,5},{5,6},{6,7},{7,0},{8,9},{9,10},{10,1... | collective-permute-start | bytes 73736 | tf_op jit(solution)/shard_map/ppermute | solution.py:27
  588.2 15.9 %collective-permute-start.15 = (f32[1,12,4,8,16]{4,3,2,1,0:T(8,128)}, f32[1,12,4,8,16]{4,3,2,1,0:T(8,128)}, u32[]{:S(2)}, u32[]{:S(2)}) collective-permute-start(f32[1,12,4,8,16]{4,3,2,1,0:T(8,128)} %pad_maximum_fusion.8), channel_id=1, source_target_pairs={{1,0},{2,1},{3,2},{4,3},{5,4},{6,5},{7,6},{0,7},{9,8},{10,9},{11,1... | collective-permute-start | bytes 73736 | tf_op jit(solution)/shard_map/ppermute | solution.py:28
  640.5 21.0 %collective-permute-start.36 = (f32[1,4,4,8,16]{4,3,2,1,0:T(8,128)S(1)}, f32[1,4,4,8,16]{4,3,2,1,0:T(8,128)S(1)}, u32[]{:S(2)}, u32[]{:S(2)}) collective-permute-start(f32[1,4,4,8,16]{4,3,2,1,0:T(8,128)S(1)} %bitcast.343), channel_id=1, source_target_pairs={{0,8},{8,16},{16,24},{24,32},{32,40},{40,48},{48,56},{56,64},{64,7... | collective-permute-start | bytes 24584 | tf_op jit(solution)/shard_map/ppermute | solution.py:27
  642.5 19.1 %collective-permute-start.37 = (f32[1,4,4,8,16]{4,3,2,1,0:T(8,128)S(1)}, f32[1,4,4,8,16]{4,3,2,1,0:T(8,128)S(1)}, u32[]{:S(2)}, u32[]{:S(2)}) collective-permute-start(f32[1,4,4,8,16]{4,3,2,1,0:T(8,128)S(1)} %bitcast.344), channel_id=1, source_target_pairs={{8,0},{16,8},{24,16},{32,24},{40,32},{48,40},{56,48},{64,56},{72,6... | collective-permute-start | bytes 24584 | tf_op jit(solution)/shard_map/ppermute | solution.py:28
  650.0 17.4 %collective-permute-start.32 = (bf16[1,4,4,8,512]{4,3,2,1,0:T(8,128)(2,1)}, bf16[1,4,4,8,512]{4,3,2,1,0:T(8,128)(2,1)S(1)}, u32[]{:S(2)}, u32[]{:S(2)}) collective-permute-start(bf16[1,4,4,8,512]{4,3,2,1,0:T(8,128)(2,1)} %bitcast.331), channel_id=1, source_target_pairs={{0,8},{8,16},{16,24},{24,32},{32,40},{40,48},{48,56},{56,64},{64,7... | collective-permute-start | bytes 393224 | tf_op jit(solution)/shard_map/ppermute | solution.py:27
  651.9 15.5 %collective-permute-start.33 = (bf16[1,4,4,8,512]{4,3,2,1,0:T(8,128)(2,1)}, bf16[1,4,4,8,512]{4,3,2,1,0:T(8,128)(2,1)S(1)}, u32[]{:S(2)}, u32[]{:S(2)}) collective-permute-start(bf16[1,4,4,8,512]{4,3,2,1,0:T(8,128)(2,1)} %bitcast.332), channel_id=1, source_target_pairs={{8,0},{16,8},{24,16},{32,24},{40,32},{48,40},{56,48},{64,56},{72,6... | collective-permute-start | bytes 393224 | tf_op jit(solution)/shard_map/ppermute | solution.py:28
  661.5 25.6 %collective-permute-start.38 = (f32[1,12,4,8,16]{4,3,2,1,0:T(8,128)S(1)}, f32[1,12,4,8,16]{4,3,2,1,0:T(8,128)}, u32[]{:S(2)}, u32[]{:S(2)}) collective-permute-start(f32[1,12,4,8,16]{4,3,2,1,0:T(8,128)S(1)} %pad_maximum_fusion.11), channel_id=1, source_target_pairs={{0,1},{1,2},{2,3},{3,4},{4,5},{5,6},{6,7},{7,0},{8,9},{9,10},{10,1... | collective-permute-start | bytes 73736 | tf_op jit(solution)/shard_map/ppermute | solution.py:27
  663.5 23.7 %collective-permute-start.39 = (f32[1,12,4,8,16]{4,3,2,1,0:T(8,128)S(1)}, f32[1,12,4,8,16]{4,3,2,1,0:T(8,128)}, u32[]{:S(2)}, u32[]{:S(2)}) collective-permute-start(f32[1,12,4,8,16]{4,3,2,1,0:T(8,128)S(1)} %pad_maximum_fusion.11), channel_id=1, source_target_pairs={{1,0},{2,1},{3,2},{4,3},{5,4},{6,5},{7,6},{0,7},{9,8},{10,9},{11,1... | collective-permute-start | bytes 73736 | tf_op jit(solution)/shard_map/ppermute | solution.py:28
  669.1 19.3 %collective-permute-start.34 = (bf16[1,12,4,8,512]{4,3,2,1,0:T(8,128)(2,1)}, bf16[1,12,4,8,512]{4,3,2,1,0:T(8,128)(2,1)}, u32[]{:S(2)}, u32[]{:S(2)}) collective-permute-start(bf16[1,12,4,8,512]{4,3,2,1,0:T(8,128)(2,1)} %pad_maximum_fusion.7), channel_id=1, source_target_pairs={{0,1},{1,2},{2,3},{3,4},{4,5},{5,6},{6,7},{7,0},{8,9},{9,10},{10,1... | collective-permute-start | bytes 1179656 | tf_op jit(solution)/shard_map/ppermute | solution.py:27
  677.1 19.3 %collective-permute-start.35 = (bf16[1,12,4,8,512]{4,3,2,1,0:T(8,128)(2,1)}, bf16[1,12,4,8,512]{4,3,2,1,0:T(8,128)(2,1)}, u32[]{:S(2)}, u32[]{:S(2)}) collective-permute-start(bf16[1,12,4,8,512]{4,3,2,1,0:T(8,128)(2,1)} %pad_maximum_fusion.7), channel_id=1, source_target_pairs={{1,0},{2,1},{3,2},{4,3},{5,4},{6,5},{7,6},{0,7},{9,8},{10,9},{11,1... | collective-permute-start | bytes 1179656 | tf_op jit(solution)/shard_map/ppermute | solution.py:28
  (46 other events, 357.4 us)
where the time goes:
time: 723 us; the launch traced here: 717 us
  starting transfers between devices  192 us (27%)
  waiting for transfers between devices  172 us (24%)
  local copies, waits for them, and re-layouts  117 us (16%)
  matrix products  99 us (14%)
  blocking collectives  93.4 us (13%)
  other arithmetic  40.5 us (6%)
    ppermute x20, starting transfers between devices, extended(): before = lax.ppermute(last, axis, up)  96 us
    ppermute x20, starting transfers between devices, extended(): after = lax.ppermute(first, axis, down)  95.5 us
    psum x1, blocking collectives, local(): square_sum = lax.psum(jnp.sum(misfit_f * misfit_f), ('shot', 'rec'))  93.4 us
    ppermute x20, waiting for transfers between devices, extended(): before = lax.ppermute(last, axis, up)  90 us
    ppermute x20, waiting for transfers between devices, extended(): after = lax.ppermute(first, axis, down)  82.1 us
    reshape x30, local copies, waits for them, and re-layouts, heads_last(): flat = field.reshape(batches, -1, HEADS, HS)  65.2 us
    dot_general x4, matrix products, pair_scores(): jnp.einsum('bhdq,bhdk->bhqk', left, right, preferred_element_type=jnp.flo...  27.7 us
    concatenate x18, other arithmetic, extended(): x = jnp.concatenate([before, x, after], axis=dim)  25.6 us
  transfers between devices with their start and end apart: 40, of which 8 were waited for; matrix products, arithmetic and copies ran while one was open for 21% of the time, Pallas kernels for 0%

commit v1 on v0

v1 whole, which is shorter than its diff:
```python
import functools
import math

import jax
import jax.numpy as jnp
from jax import lax
from jax.experimental import pallas as pl
from jax.experimental.pallas import tpu as pltpu
from jax.sharding import PartitionSpec as P

HEADS = 16
HS = 32
STEPS = 1000
D = 512
TOK = 128
HALF = 4
OWN = 4
CHUNKS = 4

sigma_low = 0.5
sigma_high = 8.0
sigma_data = 0.5
norm_eps = 1e-06
SCALE = HS ** (-0.5)
LOG2E = math.log2(math.e)
MASKED = -1e30

f32 = jnp.float32
bf16 = jnp.bfloat16
MESH = pl.DeviceIdType.MESH


def reduction_stages(n_shot, n_rec):
    digits = []
    for axis, size in ((0, n_shot), (1, n_rec)):
        stride = 2
        while stride < size:
            digits.append((axis, stride, 2))
            stride *= 2
    return [digits[i : i + 2] for i in range(0, len(digits), 2)]


def stage_peers(stage, shot, rec):
    place = [shot, rec]
    now, size = 0, 1
    for axis, stride, radix in stage:
        now = now + size * ((place[axis] // stride) % radix)
        size *= radix
    peers = []
    for k in range(1, size):
        later = (now + k) % size
        at = list(place)
        for axis, stride, radix in stage:
            digit = (place[axis] // stride) % radix
            at[axis] = at[axis] + stride * (later % radix - digit)
            later = later // radix
        peers.append((at[0], at[1]))
    return peers


def window_places(shot, rec, n_shot, n_rec):
    places = []
    near, far = shot % 2, rec % 2
    step_n, step_f = 1 - 2 * near, 1 - 2 * far
    places.append(
        (
            near,
            far,
            [(shot + step_n, rec), (shot, rec + step_f), (shot + step_n, rec + step_f)],
            [(shot - near + i % 2, 0) for i in range(4)],
        )
    )
    end = 1 - (rec % (n_rec - 1) + n_rec - 2) // (n_rec - 1)
    near = (shot + 1) % 2
    far = (1 - end) * ((rec + 1) % 2) + end * (((shot + 3) % 4) // 2)
    step_n, step_f = 1 - 2 * near, 1 - 2 * far
    move_s, move_r = 2 * end * step_f, (1 - end) * step_f
    near_shot = (shot + step_n + n_shot) % n_shot
    far_shot = (shot + move_s + n_shot) % n_shot
    diag_shot = (shot + step_n + move_s + n_shot) % n_shot
    first = shot - near - 2 * end * far + n_shot
    parts = []
    for i in range(4):
        at = (first + i % 2 + 2 * end * (i // 2)) % n_shot
        wrapped = 1 - (at + n_shot - 1) // n_shot
        parts.append((at, 2 * wrapped + end * (i // 2)))
    places.append(
        (near, far, [(near_shot, rec), (far_shot, rec + move_r), (diag_shot, rec + move_r)], parts)
    )
    return places


def split3(x):
    high = x.astype(bf16)
    rest = x - high.astype(f32)
    mid = rest.astype(bf16)
    low = (rest - mid.astype(f32)).astype(bf16)
    return high, mid, low


def dot(a, b):
    return lax.dot_general(a, b, (((1,), (0,)), ((), ())), preferred_element_type=f32)


def dot_nt(a, b):
    return lax.dot_general(a, b, (((1,), (1,)), ((), ())), preferred_element_type=f32)


def fold3(x):
    return x[:HS] + x[HS : 2 * HS] + x[2 * HS :]


def kernel(
    n_shot,
    n_rec,
    stages,
    noisy,
    misfit,
    timestep,
    segs,
    w_qkv,
    w_out,
    den,
    gui,
    noisy_v,
    misfit_v,
    noisy_t,
    misfit_t,
    stream1,
    inverse,
    wfull,
    wofull,
    wcol,
    wt,
    wot,
    nbuf,
    q3,
    k3,
    v3,
    k8t,
    v4t,
    bias,
    prob,
    pbuf,
    dbuf,
    ost,
    obuf,
    gst,
    gbuf,
    gpst,
    gpbuf,
    part,
    out_v,
    in_sem,
    w_sem,
    out_sem,
    near_s,
    near_r,
    far_s,
    far_r,
    rel_s,
    rel_r,
    o_s,
    o_r,
    g_s,
    g_r,
    gp_s,
    gp_r,
    red_s,
    red_r,
):
    shot, rec = lax.axis_index("shot"), lax.axis_index("rec")
    places = window_places(shot, rec, n_shot, n_rec)
    own, blocks, peers = [], [], []
    for near, far, partners, _ in places:
        here = 2 * far + near
        own.append(here)
        blocks.append([2 * far + 1 - near, 2 - 2 * far + near, 3 - 2 * far - near])
        peers.append(partners)
    red_peers = [peers[0]] + [stage_peers(stage, shot, rec) for stage in stages]

    noisy_in = pltpu.make_async_copy(noisy, noisy_v, in_sem.at[0])
    misfit_in = pltpu.make_async_copy(misfit, misfit_v, in_sem.at[1])
    noisy_in.start()
    misfit_in.start()
    col_in = [
        [
            pltpu.make_async_copy(
                w_qkv.at[b, :, pl.ds(pl.multiple_of(third * D + own[b] * TOK, TOK), TOK)],
                wcol.at[b, third],
                w_sem.at[3 * b + third],
            )
            for third in range(3)
        ]
        for b in range(2)
    ]
    out_in = [pltpu.make_async_copy(w_out.at[b], wofull.at[b], w_sem.at[6 + b]) for b in range(2)]
    full_in = [pltpu.make_async_copy(w_qkv.at[b], wfull.at[b], w_sem.at[8 + b]) for b in range(2)]
    for copy in col_in[0] + [out_in[0], out_in[1]] + col_in[1] + [full_in[1], full_in[0]]:
        copy.start()

    barrier = pltpu.get_barrier_semaphore()
    greeted = peers[0] + peers[1] + [peer for some in red_peers[1:] for peer in some]
    for peer in greeted:
        pl.semaphore_signal(barrier, inc=1, device_id=peer, device_id_type=MESH)

    def remote(src, dst, send, recv, peer):
        return pltpu.make_async_remote_copy(
            src_ref=src, dst_ref=dst, send_sem=send, recv_sem=recv, device_id=peer, device_id_type=MESH
        )

    rows = D // CHUNKS

    def near_copy(b):
        block = nbuf.at[b, own[b]]
        return remote(block, block, near_s.at[b], near_r.at[b], peers[b][0])

    def far_copy(b, k):
        block = nbuf.at[b, own[b], pl.ds(k * rows, rows)]
        return remote(block, block, far_s.at[b, k], far_r.at[b, k], peers[b][1])

    def relay_copy(b, k):
        block = nbuf.at[b, blocks[b][1], pl.ds(k * rows, rows)]
        return remote(block, block, rel_s.at[b, k], rel_r.at[b, k], peers[b][0])

    def o_copy(b, m):
        return remote(
            ost.at[b, blocks[b][m]], obuf.at[b, own[b]], o_s.at[b, m], o_r.at[b, m], peers[b][m]
        )

    def g_copy(b, m):
        return remote(
            gst.at[b, blocks[b][m]], gbuf.at[b, own[b]], g_s.at[b, m], g_r.at[b, m], peers[b][m]
        )

    def gp_copy(b, m, h):
        return remote(
            gpst.at[b, h, blocks[b][m]],
            gpbuf.at[b, own[b], h],
            gp_s.at[b, m, h],
            gp_r.at[b, m, h],
            peers[b][m],
        )

    def red_copy(stage, k):
        return remote(
            part.at[stage, 0],
            part.at[stage, k + 1],
            red_s.at[stage, k],
            red_r.at[stage, k],
            red_peers[stage][k],
        )

    def red_send(stage, value):
        part[stage, 0] = value
        for k in range(len(red_peers[stage])):
            red_copy(stage, k).start()

    def red_take(stage):
        total = part[stage, 0]
        for k in range(len(red_peers[stage])):
            red_copy(stage, k).wait_recv()
            total = total + part[stage, k + 1]
        return total

    fraction = jnp.full((1, TOK), timestep[0].astype(f32), f32) / (STEPS - 1)
    noise_level = sigma_low * jnp.exp(fraction * math.log(sigma_high / sigma_low))
    spread = noise_level * noise_level + sigma_data * sigma_data
    c_skip = sigma_data * sigma_data / spread
    c_out = noise_level * sigma_data * lax.rsqrt(spread)
    c_in = lax.rsqrt(spread)

    def normalise(b, stream):
        inv = lax.rsqrt(jnp.sum(stream * stream, axis=0, keepdims=True) * (1.0 / D) + norm_eps)
        inverse[b] = inv
        nbuf[b, own[b]] = (stream * inv).astype(bf16)

    noisy_in.wait()
    noisy_t[...] = noisy_v[...].astype(f32).T
    normalise(0, c_in * noisy_t[...])
    pl.semaphore_wait(barrier, len(greeted))

    def gather_start(b):
        for k in range(CHUNKS):
            far_copy(b, k).start()
        near_copy(b).start()

    def prepare_weights(b):
        for third in range(3):
            col_in[b][third].wait()
            wt[b, third * TOK : (third + 1) * TOK, :] = wcol[b, third].T

    def project(b, block):
        packed = dot(wt[b], nbuf[b, block])
        q = split3(packed[:TOK] * (SCALE * LOG2E))
        k = split3(packed[TOK : 2 * TOK])
        v = split3(packed[2 * TOK :])
        zero = jnp.zeros((HS, TOK), bf16)
        for h in range(OWN):
            at = slice(h * HS, (h + 1) * HS)
            kh, km, kl = [x[at] for x in k]
            vh, vm, vl = [x[at] for x in v]
            q3[b, h, block] = jnp.concatenate([x[at] for x in q], axis=0)
            k3[b, h, block] = jnp.concatenate([kh, km, kl], axis=0)
            v3[b, h, block] = jnp.concatenate([vh, vm, vl], axis=0)
            k8t[b, h, block] = jnp.concatenate([kh, kh, kh, km, km, kl, km, kl], axis=0).T
            v4t[b, h, block] = jnp.concatenate([vh, vm, vl, zero], axis=0).T

    def make_bias(b):
        parts = places[b][3]
        ids = []
        for at, mark in parts:
            ids.append([segs[HALF * at + s] * 4 + mark for s in range(HALF)])
        lane = lax.broadcasted_iota(jnp.int32, (HS, TOK), 1)
        for j in range(4):
            line = jnp.where(
                lane < 64,
                jnp.where(lane < 32, ids[j][0], ids[j][1]),
                jnp.where(lane < 96, ids[j][2], ids[j][3]),
            )
            for i in range(4):
                for s in range(HALF):
                    at = i * TOK + s * HS
                    bias[b, j, at : at + HS, :] = jnp.where(line == ids[i][s], 0.0, MASKED)

    def gather_rest(b):
        project(b, own[b])
        make_bias(b)
        near_copy(b).wait_recv()
        project(b, blocks[b][0])
        for k in range(CHUNKS):
            far_copy(b, k).wait_recv()
            relay_copy(b, k).start()
        project(b, blocks[b][1])

    def gather_last(b):
        for k in range(CHUNKS):
            relay_copy(b, k).wait_recv()
        project(b, blocks[b][2])

    def attention(b, h, j):
        q = q3[b, h, j]
        qh, qm, ql = q[:HS], q[HS : 2 * HS], q[2 * HS :]
        q8 = jnp.concatenate([qh, qm, ql, qh, qm, qh, ql, qm], axis=0)
        scores = dot(k8t[b, h].reshape(4 * TOK, 8 * HS), q8) + bias[b, j]
        shifted = jnp.exp2(scores - jnp.max(scores, axis=0, keepdims=True))
        return shifted * (1.0 / jnp.sum(shifted, axis=0, keepdims=True))

    def wide(ref, b, h):
        return jnp.concatenate([ref[b, h, i] for i in range(4)], axis=1)

    def wide_pairs(ref):
        return jnp.concatenate([ref[i] for i in range(4)], axis=1)

    def score_grad(b, h, j, p):
        g = gbuf[b, j, pl.ds(pl.multiple_of(h * HS, HS), HS), :]
        g4 = jnp.concatenate([g, g, g, g], axis=0)
        grad_prob = dot(v4t[b, h].reshape(4 * TOK, 4 * HS), g4)
        row_dot = jnp.sum(p * grad_prob, axis=0, keepdims=True)
        return (p * (grad_prob - row_dot)).astype(bf16)

    def head_back(b, h):
        pw, dw = wide_pairs(pbuf), wide_pairs(dbuf)
        g = jnp.concatenate(
            [gbuf[b, i, pl.ds(pl.multiple_of(h * HS, HS), HS), :] for i in range(4)], axis=1
        )
        grad_q = (fold3(dot(wide(k3, b, h), dw)) * SCALE).astype(bf16)
        grad_k = (fold3(dot_nt(wide(q3, b, h), dw)) * (1.0 / LOG2E)).astype(bf16)
        grad_v = dot_nt(g, pw).astype(bf16)
        for j in range(4):
            at = slice(j * TOK, (j + 1) * TOK)
            gpst[b, h, j] = jnp.concatenate([grad_q[:, at], grad_k[:, at], grad_v[:, at]], axis=0)
        for m in (2, 1, 0):
            gp_copy(b, m, h).start()
        gpbuf[b, own[b], h] = gpst[b, h, own[b]]

    def packed_back(b, stream, grad_next):
        def arrive(h, carry):
            for m in range(3):
                gp_copy(b, m, h).wait_recv()
            return carry

        lax.fori_loop(0, OWN, arrive, 0)
        pieces = []
        for third in range(3):
            for i in range(4):
                for h in range(OWN):
                    pieces.append(gpbuf[b, i, h, third * HS : (third + 1) * HS, :])
        grad_normed = dot(wfull[b], jnp.concatenate(pieces, axis=0))
        inv = inverse[b]
        normed = stream * inv
        mean = jnp.sum(grad_normed * normed, axis=0, keepdims=True) * (1.0 / D)
        return grad_next + inv * (grad_normed - normed * mean)

    def send_grads(b, grad_next):
        grads = dot(wofull[b], grad_next.astype(bf16)).astype(bf16)
        gst[b] = grads.reshape(4, TOK, TOK)
        for m in (2, 1, 0):
            g_copy(b, m).start()
        gbuf[b, own[b]] = gst[b, own[b]]

    def branch(b):
        return dot(wot[b], obuf[b].reshape(D, TOK))

    gather_start(0)
    misfit_in.wait()
    misfit_f = misfit_v[...].astype(f32)
    squares = jnp.sum(misfit_f * misfit_f, axis=0, keepdims=True)
    squares = squares[:, :128] + squares[:, 128:256] + squares[:, 256:384] + squares[:, 384:]
    red_send(0, jnp.broadcast_to(squares, (8, 128)))
    prepare_weights(0)
    gather_rest(0)
    misfit_t[...] = misfit_f.T
    stage = 0
    red_send(1, red_take(0))
    stage = 1
    gather_last(0)
    for m in (2, 1, 0, None):
        block = own[0] if m is None else blocks[0][m]
        for h in range(OWN):
            p = attention(0, h, block)
            prob[h, block] = p
            o = fold3(dot(wide(v3, 0, h), p.astype(bf16)))
            ost[0, block, h * HS : (h + 1) * HS, :] = o.astype(bf16)
        if m is None:
            obuf[0, own[0]] = ost[0, own[0]]
        else:
            o_copy(0, m).start()
        if stage < len(stages):
            red_send(stage + 1, red_take(stage))
            stage += 1
    while stage < len(stages):
        red_send(stage + 1, red_take(stage))
        stage += 1
    prepare_weights(1)
    for b in range(2):
        out_in[b].wait()
    wot[0] = wofull[0].T
    square_sum = jnp.sum(red_take(stage)[:1], axis=1, keepdims=True)
    entries = float(n_shot * n_rec * TOK * D)
    misfit_scale = lax.rsqrt(square_sum / entries + norm_eps)
    send_grads(1, c_out * (misfit_t[...] * misfit_scale))
    for m in range(3):
        o_copy(0, m).wait_recv()
    stream1[...] = c_in * noisy_t[...] + branch(0)
    normalise(1, stream1[...])

    gather_start(1)
    gather_rest(1)
    wot[1] = wofull[1].T
    for m in range(3):
        g_copy(1, m).wait_recv()
    gather_last(1)

    def second(h, carry):
        for j in range(4):
            p = attention(1, h, j)
            pbuf[j] = p.astype(bf16)
            dbuf[j] = score_grad(1, h, j, p)
        head_back(1, h)
        o = fold3(dot(wide(v3, 1, h), wide_pairs(pbuf))).astype(bf16)
        for j in range(4):
            ost[1, j, pl.ds(pl.multiple_of(h * HS, HS), HS), :] = o[:, j * TOK : (j + 1) * TOK]
        return carry

    lax.fori_loop(0, OWN, second, 0)
    for m in (2, 1, 0):
        o_copy(1, m).start()
    obuf[1, own[1]] = ost[1, own[1]]
    for b in (1, 0):
        full_in[b].wait()
    weight = misfit_t[...] * misfit_scale
    grad1 = packed_back(1, stream1[...], c_out * weight)
    send_grads(0, grad1)
    for m in range(3):
        o_copy(1, m).wait_recv()
    final = stream1[...] + branch(1)
    out_v[0] = (c_skip * noisy_t[...] + c_out * final).T.astype(bf16)
    den_out = pltpu.make_async_copy(out_v.at[0], den, out_sem.at[0])
    den_out.start()
    stream1[...] = grad1
    for m in range(3):
        g_copy(0, m).wait_recv()

    def first(h, carry):
        for j in range(4):
            p = prob[h, j]
            pbuf[j] = p.astype(bf16)
            dbuf[j] = score_grad(0, h, j, p)
        head_back(0, h)
        return carry

    lax.fori_loop(0, OWN, first, 0)
    grad0 = packed_back(0, c_in * noisy_t[...], stream1[...])
    weight = misfit_t[...] * misfit_scale
    out_v[1] = (c_skip * weight + c_in * grad0).T.astype(bf16)
    gui_out = pltpu.make_async_copy(out_v.at[1], gui, out_sem.at[1])
    gui_out.start()

    for b in range(2):
        near_copy(b).wait_send()
        for k in range(CHUNKS):
            far_copy(b, k).wait_send()
            relay_copy(b, k).wait_send()
        for m in range(3):
            o_copy(b, m).wait_send()
            g_copy(b, m).wait_send()

        def leave(h, carry, b=b):
            for m in range(3):
                gp_copy(b, m, h).wait_send()
            return carry

        lax.fori_loop(0, OWN, leave, 0)
    for stage in range(len(red_peers)):
        for k in range(len(red_peers[stage])):
            red_copy(stage, k).wait_send()
    den_out.wait()
    gui_out.wait()


def local(n_shot, n_rec, noisy, misfit, timestep, segment_ids, w_qkv, w_out):
    stages = reduction_stages(n_shot, n_rec)
    shape = noisy.shape
    any_space = pl.BlockSpec(memory_space=pl.ANY)
    scalars = pl.BlockSpec(memory_space=pltpu.SMEM)
    dma = pltpu.SemaphoreType.DMA
    scratch = [
        pltpu.VMEM((TOK, D), bf16),
        pltpu.VMEM((TOK, D), bf16),
        pltpu.VMEM((D, TOK), f32),
        pltpu.VMEM((D, TOK), f32),
        pltpu.VMEM((D, TOK), f32),
        pltpu.VMEM((2, 1, TOK), f32),
        pltpu.VMEM((2, D, 3 * D), bf16),
        pltpu.VMEM((2, D, D), bf16),
        pltpu.VMEM((2, 3, D, TOK), bf16),
        pltpu.VMEM((2, 3 * TOK, D), bf16),
        pltpu.VMEM((2, D, D), bf16),
        pltpu.VMEM((2, 4, D, TOK), bf16),
        pltpu.VMEM((2, OWN, 4, 3 * HS, TOK), bf16),
        pltpu.VMEM((2, OWN, 4, 3 * HS, TOK), bf16),
        pltpu.VMEM((2, OWN, 4, 3 * HS, TOK), bf16),
        pltpu.VMEM((2, OWN, 4, TOK, 8 * HS), bf16),
        pltpu.VMEM((2, OWN, 4, TOK, 4 * HS), bf16),
        pltpu.VMEM((2, 4, 4 * TOK, TOK), f32),
        pltpu.VMEM((OWN, 4, 4 * TOK, TOK), f32),
        pltpu.VMEM((4, 4 * TOK, TOK), bf16),
        pltpu.VMEM((4, 4 * TOK, TOK), bf16),
        pltpu.VMEM((2, 4, TOK, TOK), bf16),
        pltpu.VMEM((2, 4, TOK, TOK), bf16),
        pltpu.VMEM((2, 4, TOK, TOK), bf16),
        pltpu.VMEM((2, 4, TOK, TOK), bf16),
        pltpu.VMEM((2, OWN, 4, 3 * HS, TOK), bf16),
        pltpu.VMEM((2, 4, OWN, 3 * HS, TOK), bf16),
        pltpu.VMEM((len(stages) + 1, 4, 8, 128), f32),
        pltpu.VMEM((2, TOK, D), bf16),
        dma((2,)),
        dma((10,)),
        dma((2,)),
        dma((2,)),
        dma((2,)),
        dma((2, CHUNKS)),
        dma((2, CHUNKS)),
        dma((2, CHUNKS)),
        dma((2, CHUNKS)),
        dma((2, 3)),
        dma((2, 3)),
        dma((2, 3)),
        dma((2, 3)),
        dma((2, 3, OWN)),
        dma((2, 3, OWN)),
        dma((len(stages) + 1, 3)),
        dma((len(stages) + 1, 3)),
    ]
    den, gui = pl.pallas_call(
        functools.partial(kernel, n_shot, n_rec, stages),
        out_shape=[jax.ShapeDtypeStruct((TOK, D), bf16)] * 2,
        in_specs=[any_space, any_space, scalars, scalars, any_space, any_space],
        out_specs=[any_space, any_space],
        scratch_shapes=scratch,
        compiler_params=pltpu.CompilerParams(
            collective_id=0, has_side_effects=True, vmem_limit_bytes=62 * 1024 * 1024
        ),
        cost_estimate=pl.CostEstimate(
            flops=2_000_000_000, bytes_accessed=6_000_000, transcendentals=2_000_000
        ),
        name="window_pair",
    )(noisy.reshape(TOK, D), misfit.reshape(TOK, D), timestep, segment_ids, w_qkv, w_out)
    return den.reshape(shape), gui.reshape(shape)


def solution(mesh):
    tokens = P(None, "shot", "rec", None, None)
    return jax.shard_map(
        functools.partial(local, mesh.shape["shot"], mesh.shape["rec"]),
        mesh=mesh,
        in_specs=(tokens, tokens, P(), P(), P(), P()),
        out_specs=(tokens, tokens),
        check_vma=False,
    )
```

time: 723 us -> 87.4 us (0.12)
  the two profiles are of different devices: /device:TPU:6 before, /device:TPU:48 now
where the time goes in v1:
time: 87.4 us; the launch traced here: 87.2 us
  Pallas kernels  82.8 us (95%)
  local copies, waits for them, and re-layouts  3.14 us (4%)
  between operations  1.29 us (1%)
    pallas_call x1, Pallas kernels, local(): pl.pallas_call(functools.partial(kernel, n_shot, n_rec, stages), out_shap...  82.8 us
    unnamed x2, local copies, waits for them, and re-layouts  3.14 us

profile of v1, /device:TPU:48, one launch (start us, length us, event | category | flops | bytes accessed | tf_op | source)
XLA Modules:
  0.0 87.2 jit_solution(16360208523245458328)
XLA Ops:
  1.3 82.8 %window_pair.1 = (bf16[128,512]{1,0:T(8,128)(2,1)}, bf16[128,512]{1,0:T(8,128)(2,1)}) custom-call(bf16[128,512]{1,0:T(8,128)(2,1)} %bitcast.6, bf16[128,512]{1,0:T(8,128)(2,1)} %bitcast.7, s32[1]{0:T(128)S(6)} %copy.10.timestep, s32[256]{0:T(256)} %segs.1, bf16[2,512,1536]{2,1,0:T(8,128)(2,1)} %w_qkv.1, bf16[2,512,512]{2,1,0:T(8,128)(2,1)} %w_out.1), custom_call_target="tpu_custom_call" | custom-call | flops 2000000000 | bytes 6000000 | tf_op jit(solution)/shard_map/window_pair/pallas_call | solution.py:576
  84.1 1.6 %copy.11 = bf16[1,4,4,8,512]{4,3,2,1,0:T(8,128)(2,1)} copy(bf16[1,4,4,8,512]{4,3,2,1,0:T(8,128)(2,1)} %bitcast.5) | data formatting | bytes 262144
  85.7 1.6 %copy.12 = bf16[1,4,4,8,512]{4,3,2,1,0:T(8,128)(2,1)} copy(bf16[1,4,4,8,512]{4,3,2,1,0:T(8,128)(2,1)} %bitcast.4) | data formatting | bytes 262144

commit v2 on v1

--- a/solution.py
+++ b/solution.py
@@ -15,6 +15,7 @@
 TOK = 128
 HALF = 4
 OWN = 4
+GROUPS = 64
 CHUNKS = 4
 
 sigma_low = 0.5
@@ -24,6 +25,7 @@
 SCALE = HS ** (-0.5)
 LOG2E = math.log2(math.e)
 MASKED = -1e30
+VMEM_LIMIT = 62 * 1024 * 1024
 
 f32 = jnp.float32
 bf16 = jnp.bfloat16
@@ -123,7 +125,6 @@
     den,
     gui,
     noisy_v,
-    misfit_v,
     noisy_t,
     misfit_t,
     stream1,
@@ -134,15 +135,18 @@
     wt,
     wot,
     nbuf,
+    mbuf,
     q3,
     k3,
     v3,
     k8t,
     v4t,
-    bias,
+    mrow,
     prob,
     pbuf,
     dbuf,
+    sbuf,
+    tbuf,
     ost,
     obuf,
     gst,
@@ -160,6 +164,8 @@
     far_r,
     rel_s,
     rel_r,
+    mis_s,
+    mis_r,
     o_s,
     o_r,
     g_s,
@@ -177,10 +183,19 @@
         own.append(here)
         blocks.append([2 * far + 1 - near, 2 - 2 * far + near, 3 - 2 * far - near])
         peers.append(partners)
+    def block_at(b, i):
+        near, far = places[b][:2]
+        return 2 * (far + (i // 2) * (1 - 2 * far)) + near + (i % 2) * (1 - 2 * near)
+
     red_peers = [peers[0]] + [stage_peers(stage, shot, rec) for stage in stages]
 
+    barrier = pltpu.get_barrier_semaphore()
+    greeted = peers[0] + peers[1] + [peer for some in red_peers[1:] for peer in some]
+    for peer in greeted:
+        pl.semaphore_signal(barrier, inc=1, device_id=peer, device_id_type=MESH)
+
     noisy_in = pltpu.make_async_copy(noisy, noisy_v, in_sem.at[0])
-    misfit_in = pltpu.make_async_copy(misfit, misfit_v, in_sem.at[1])
+    misfit_in = pltpu.make_async_copy(misfit, mbuf.at[own[1]], in_sem.at[1])
     noisy_in.start()
     misfit_in.start()
     col_in = [
@@ -196,13 +211,8 @@
     ]
     out_in = [pltpu.make_async_copy(w_out.at[b], wofull.at[b], w_sem.at[6 + b]) for b in range(2)]
     full_in = [pltpu.make_async_copy(w_qkv.at[b], wfull.at[b], w_sem.at[8 + b]) for b in range(2)]
-    for copy in col_in[0] + [out_in[0], out_in[1]] + col_in[1] + [full_in[1], full_in[0]]:
+    for copy in col_in[0]:
         copy.start()
-
-    barrier = pltpu.get_barrier_semaphore()
-    greeted = peers[0] + peers[1] + [peer for some in red_peers[1:] for peer in some]
-    for peer in greeted:
-        pl.semaphore_signal(barrier, inc=1, device_id=peer, device_id_type=MESH)
 
     def remote(src, dst, send, recv, peer):
         return pltpu.make_async_remote_copy(
@@ -223,14 +233,18 @@
         block = nbuf.at[b, blocks[b][1], pl.ds(k * rows, rows)]
         return remote(block, block, rel_s.at[b, k], rel_r.at[b, k], peers[b][0])
 
+    def misfit_copy(m):
+        block = mbuf.at[blocks[1][1] if m == 2 else own[1]]
+        return remote(block, block, mis_s.at[m], mis_r.at[m], peers[1][m % 2])
+
     def o_copy(b, m):
         return remote(
             ost.at[b, blocks[b][m]], obuf.at[b, own[b]], o_s.at[b, m], o_r.at[b, m], peers[b][m]
         )
 
-    def g_copy(b, m):
+    def g_copy(m):
         return remote(
-            gst.at[b, blocks[b][m]], gbuf.at[b, own[b]], g_s.at[b, m], g_r.at[b, m], peers[b][m]
+            gst.at[blocks[0][m]], gbuf.at[0, own[0]], g_s.at[m], g_r.at[m], peers[0][m]
         )
 
     def gp_copy(b, m, h):
@@ -296,6 +310,9 @@
         k = split3(packed[TOK : 2 * TOK])
         v = split3(packed[2 * TOK :])
         zero = jnp.zeros((HS, TOK), bf16)
+        lane = lax.broadcasted_iota(jnp.int32, (GROUPS, TOK), 1)
+        row = lax.broadcasted_iota(jnp.int32, (GROUPS, TOK), 0)
+        member = jnp.where(row == HALF * block + lane // HS, 1.0, 0.0).astype(bf16)
         for h in range(OWN):
             at = slice(h * HS, (h + 1) * HS)
             kh, km, kl = [x[at] for x in k]
@@ -303,67 +320,69 @@
             q3[b, h, block] = jnp.concatenate([x[at] for x in q], axis=0)
             k3[b, h, block] = jnp.concatenate([kh, km, kl], axis=0)
             v3[b, h, block] = jnp.concatenate([vh, vm, vl], axis=0)
-            k8t[b, h, block] = jnp.concatenate([kh, kh, kh, km, km, kl, km, kl], axis=0).T
+            k8t[b, h, block] = jnp.concatenate([kh, kh, kh, km, km, kl, member], axis=0).T
             v4t[b, h, block] = jnp.concatenate([vh, vm, vl, zero], axis=0).T
 
-    def make_bias(b):
-        parts = places[b][3]
-        ids = []
-        for at, mark in parts:
-            ids.append([segs[HALF * at + s] * 4 + mark for s in range(HALF)])
-        lane = lax.broadcasted_iota(jnp.int32, (HS, TOK), 1)
+    def make_mask(b):
+        ids = [[segs[HALF * at + s] * 4 + mark for s in range(HALF)] for at, mark in places[b][3]]
+        lane = lax.broadcasted_iota(jnp.int32, (GROUPS, TOK), 1)
+        row = lax.broadcasted_iota(jnp.int32, (GROUPS, TOK), 0)
+        group_id = jnp.full((GROUPS, TOK), -1, jnp.int32)
+        for g in range(4 * HALF):
+            group_id = jnp.where(row == g, ids[g // HALF][g % HALF], group_id)
         for j in range(4):
             line = jnp.where(
                 lane < 64,
                 jnp.where(lane < 32, ids[j][0], ids[j][1]),
                 jnp.where(lane < 96, ids[j][2], ids[j][3]),
             )
-            for i in range(4):
-                for s in range(HALF):
-                    at = i * TOK + s * HS
-                    bias[b, j, at : at + HS, :] = jnp.where(line == ids[i][s], 0.0, MASKED)
-
-    def gather_rest(b):
-        project(b, own[b])
-        make_bias(b)
-        near_copy(b).wait_recv()
-        project(b, blocks[b][0])
+            apart = (line != group_id) & (row < 4 * HALF)
+            mrow[b, j] = jnp.where(apart, MASKED, 0.0).astype(bf16)
+
+    def relay(b):
         for k in range(CHUNKS):
             far_copy(b, k).wait_recv()
             relay_copy(b, k).start()
-        project(b, blocks[b][1])
-
-    def gather_last(b):
+
+    def relayed(b):
         for k in range(CHUNKS):
             relay_copy(b, k).wait_recv()
-        project(b, blocks[b][2])
-
-    def attention(b, h, j):
-        q = q3[b, h, j]
-        qh, qm, ql = q[:HS], q[HS : 2 * HS], q[2 * HS :]
-        q8 = jnp.concatenate([qh, qm, ql, qh, qm, qh, ql, qm], axis=0)
-        scores = dot(k8t[b, h].reshape(4 * TOK, 8 * HS), q8) + bias[b, j]
+
+    def scores_of(b, h, side):
+        parts = []
+        for i in range(2):
+            q = q3[b, h, 2 * side + i]
+            qh, qm, ql = q[:HS], q[HS : 2 * HS], q[2 * HS :]
+            parts.append(
+                jnp.concatenate([qh, qm, ql, qh, qm, qh, mrow[b, 2 * side + i]], axis=0)
+            )
+        return dot(k8t[b, h].reshape(4 * TOK, 8 * HS), jnp.concatenate(parts, axis=1))
+
+    def softmax(scores):
         shifted = jnp.exp2(scores - jnp.max(scores, axis=0, keepdims=True))
         return shifted * (1.0 / jnp.sum(shifted, axis=0, keepdims=True))
 
     def wide(ref, b, h):
         return jnp.concatenate([ref[b, h, i] for i in range(4)], axis=1)
 
-    def wide_pairs(ref):
-        return jnp.concatenate([ref[i] for i in range(4)], axis=1)
-
-    def score_grad(b, h, j, p):
-        g = gbuf[b, j, pl.ds(pl.multiple_of(h * HS, HS), HS), :]
-        g4 = jnp.concatenate([g, g, g, g], axis=0)
-        grad_prob = dot(v4t[b, h].reshape(4 * TOK, 4 * HS), g4)
+    def head_rows(h):
+        return pl.ds(pl.multiple_of(h * HS, HS), HS)
+
+    def prob_grad(b, h, side):
+        parts = []
+        for i in range(2):
+            g = gbuf[b, 2 * side + i, head_rows(h), :]
+            parts.append(jnp.concatenate([g, g, g, g], axis=0))
+        return dot(v4t[b, h].reshape(4 * TOK, 4 * HS), jnp.concatenate(parts, axis=1))
+
+    def score_grad(p, grad_prob):
         row_dot = jnp.sum(p * grad_prob, axis=0, keepdims=True)
         return (p * (grad_prob - row_dot)).astype(bf16)
 
     def head_back(b, h):
-        pw, dw = wide_pairs(pbuf), wide_pairs(dbuf)
-        g = jnp.concatenate(
-            [gbuf[b, i, pl.ds(pl.multiple_of(h * HS, HS), HS), :] for i in range(4)], axis=1
-        )
+        pw = jnp.concatenate([pbuf[b, h, 0], pbuf[b, h, 1]], axis=1)
+        dw = jnp.concatenate([dbuf[h, 0], dbuf[h, 1]], axis=1)
+        g = jnp.concatenate([gbuf[b, i, head_rows(h), :] for i in range(4)], axis=1)
         grad_q = (fold3(dot(wide(k3, b, h), dw)) * SCALE).astype(bf16)
         grad_k = (fold3(dot_nt(wide(q3, b, h), dw)) * (1.0 / LOG2E)).astype(bf16)
         grad_v = dot_nt(g, pw).astype(bf16)
@@ -373,6 +392,10 @@
         for m in (2, 1, 0):
             gp_copy(b, m, h).start()
         gpbuf[b, own[b], h] = gpst[b, h, own[b]]
+        if b == 1:
+            o = fold3(dot(wide(v3, b, h), pw)).astype(bf16)
+            for j in range(4):
+                ost[b, j, head_rows(h), :] = o[:, j * TOK : (j + 1) * TOK]
 
     def packed_back(b, stream, grad_next):
         def arrive(h, carry):
@@ -392,78 +415,156 @@
         mean = jnp.sum(grad_normed * normed, axis=0, keepdims=True) * (1.0 / D)
         return grad_next + inv * (grad_normed - normed * mean)
 
-    def send_grads(b, grad_next):
-        grads = dot(wofull[b], grad_next.astype(bf16)).astype(bf16)
-        gst[b] = grads.reshape(4, TOK, TOK)
+    def send_grads(grad_next):
+        grads = dot(wofull[0], grad_next.astype(bf16)).astype(bf16)
+        gst[...] = grads.reshape(4, TOK, TOK)
         for m in (2, 1, 0):
-            g_copy(b, m).start()
-        gbuf[b, own[b]] = gst[b, own[b]]
+            g_copy(m).start()
+        gbuf[0, own[0]] = gst[own[0]]
+
+    def second_grads(block):
+        weight = mbuf[block].astype(f32) * jnp.broadcast_to(misfit_scale, (1, D))
+        grad_next = (jnp.concatenate([c_out] * 4, axis=1) * weight).astype(bf16)
+        rows = wofull[1, pl.ds(pl.multiple_of(own[1] * TOK, TOK), TOK), :]
+        gbuf[1, block] = dot_nt(rows, grad_next).astype(bf16)
 
     def branch(b):
         return dot(wot[b], obuf[b].reshape(D, TOK))
 
+    def forward(stage):
+        if stage < len(stages):
+            red_send(stage + 1, red_take(stage))
+
     gather_start(0)
     misfit_in.wait()
-    misfit_f = misfit_v[...].astype(f32)
+    misfit_copy(1).start()
+    misfit_copy(0).start()
+    misfit_f = mbuf[own[1]].astype(f32)
     squares = jnp.sum(misfit_f * misfit_f, axis=0, keepdims=True)
     squares = squares[:, :128] + squares[:, 128:256] + squares[:, 256:384] + squares[:, 384:]
     red_send(0, jnp.broadcast_to(squares, (8, 128)))
+    out_in[0].start()
     prepare_weights(0)
-    gather_rest(0)
-    misfit_t[...] = misfit_f.T
-    stage = 0
-    red_send(1, red_take(0))
-    stage = 1
-    gather_last(0)
-    for m in (2, 1, 0, None):
-        block = own[0] if m is None else blocks[0][m]
-        for h in range(OWN):
-            p = attention(0, h, block)
-            prob[h, block] = p
-            o = fold3(dot(wide(v3, 0, h), p.astype(bf16)))
-            ost[0, block, h * HS : (h + 1) * HS, :] = o.astype(bf16)
-        if m is None:
-            obuf[0, own[0]] = ost[0, own[0]]
-        else:
-            o_copy(0, m).start()
-        if stage < len(stages):
-            red_send(stage + 1, red_take(stage))
-            stage += 1
-    while stage < len(stages):
-        red_send(stage + 1, red_take(stage))
-        stage += 1
+
+    def project_first(i, carry):
+        @pl.when(i == 1)
+        def _():
+            make_mask(0)
+            misfit_t[...] = mbuf[own[1]].astype(f32).T
+            relay(0)
+            near_copy(0).wait_recv()
+            out_in[1].start()
+            for copy in col_in[1]:
+                copy.start()
+
+        @pl.when(i == 2)
+        def _():
+            forward(0)
+
+        @pl.when(i == 3)
+        def _():
+            out_in[0].wait()
+            wot[0] = wofull[0].T
+            relayed(0)
+
+        project(0, block_at(0, i))
+        return carry
+
+    lax.fori_loop(0, 4, project_first, 0)
+    own_side = own[0] // 2
+
+    def first_place(i):
+        return i % OWN, own_side + (1 - i // OWN) * (1 - 2 * own_side)
+
+    sbuf[0] = scores_of(0, *first_place(0))
+
+    def first_ahead(i, carry):
+        h, side = first_place(i)
+        sbuf[(i + 1) % 2] = scores_of(0, *first_place((i + 1) % (2 * OWN)))
+        p = softmax(sbuf[i % 2])
+        prob[h, side] = p
+        p = p.astype(bf16)
+        pbuf[0, h, side] = p
+        o = fold3(dot(wide(v3, 0, h), p)).astype(bf16)
+        for j in range(2):
+            ost[0, 2 * side + j, head_rows(h), :] = o[:, j * TOK : (j + 1) * TOK]
+
+        @pl.when(i == 1)
+        def _():
+            forward(1)
+
+        @pl.when(i == 3)
+        def _():
+            o_copy(0, 2).start()
+            o_copy(0, 1).start()
+            misfit_copy(1).wait_recv()
+            misfit_copy(2).start()
+
+        @pl.when(i == 5)
+        def _():
+            forward(2)
+
+        return carry
+
+    lax.fori_loop(0, 2 * OWN, first_ahead, 0)
+    o_copy(0, 0).start()
+    obuf[0, own[0]] = ost[0, own[0]]
     prepare_weights(1)
-    for b in range(2):
-        out_in[b].wait()
-    wot[0] = wofull[0].T
-    square_sum = jnp.sum(red_take(stage)[:1], axis=1, keepdims=True)
-    entries = float(n_shot * n_rec * TOK * D)
-    misfit_scale = lax.rsqrt(square_sum / entries + norm_eps)
-    send_grads(1, c_out * (misfit_t[...] * misfit_scale))
+    forward(3)
     for m in range(3):
         o_copy(0, m).wait_recv()
     stream1[...] = c_in * noisy_t[...] + branch(0)
     normalise(1, stream1[...])
 
     gather_start(1)
-    gather_rest(1)
-    wot[1] = wofull[1].T
-    for m in range(3):
-        g_copy(1, m).wait_recv()
-    gather_last(1)
-
-    def second(h, carry):
-        for j in range(4):
-            p = attention(1, h, j)
-            pbuf[j] = p.astype(bf16)
-            dbuf[j] = score_grad(1, h, j, p)
-        head_back(1, h)
-        o = fold3(dot(wide(v3, 1, h), wide_pairs(pbuf))).astype(bf16)
-        for j in range(4):
-            ost[1, j, pl.ds(pl.multiple_of(h * HS, HS), HS), :] = o[:, j * TOK : (j + 1) * TOK]
+    make_mask(1)
+    full_in[1].start()
+    square_sum = jnp.sum(red_take(len(stages))[:1], axis=1, keepdims=True)
+    entries = float(n_shot * n_rec * TOK * D)
+    misfit_scale = lax.rsqrt(square_sum / entries + norm_eps)
+    out_in[1].wait()
+    misfit_copy(0).wait_recv()
+    misfit_copy(2).wait_recv()
+
+    def project_second(i, carry):
+        @pl.when(i == 1)
+        def _():
+            near_copy(1).wait_recv()
+
+        @pl.when(i == 2)
+        def _():
+            relay(1)
+
+        @pl.when(i == 3)
+        def _():
+            wot[1] = wofull[1].T
+            full_in[0].start()
+            relayed(1)
+
+        second_grads(block_at(1, i))
+        project(1, block_at(1, i))
         return carry
 
-    lax.fori_loop(0, OWN, second, 0)
+    lax.fori_loop(0, 4, project_second, 0)
+    sbuf[0] = scores_of(1, 0, 0)
+    tbuf[0] = prob_grad(1, 0, 0)
+
+    def second(i, carry):
+        h, side = i // 2, i % 2
+        later = (i + 1) % (2 * OWN)
+        sbuf[(i + 1) % 2] = scores_of(1, later // 2, later % 2)
+        tbuf[(i + 1) % 2] = prob_grad(1, later // 2, later % 2)
+        p = softmax(sbuf[i % 2])
+        pbuf[1, h, side] = p.astype(bf16)
+        dbuf[h, side] = score_grad(p, tbuf[i % 2])
+
+        @pl.when(side == 1)
+        def _():
+            head_back(1, h)
+
+        return carry
+
+    lax.fori_loop(0, 2 * OWN, second, 0)
     for m in (2, 1, 0):
         o_copy(1, m).start()
     obuf[1, own[1]] = ost[1, own[1]]
@@ -471,7 +572,7 @@
         full_in[b].wait()
     weight = misfit_t[...] * misfit_scale
     grad1 = packed_back(1, stream1[...], c_out * weight)
-    send_grads(0, grad1)
+    send_grads(grad1)
     for m in range(3):
         o_copy(1, m).wait_recv()
     final = stream1[...] + branch(1)
@@ -479,18 +580,21 @@
     den_out = pltpu.make_async_copy(out_v.at[0], den, out_sem.at[0])
     den_out.start()
     stream1[...] = grad1
-    for m in range(3):
-        g_copy(0, m).wait_recv()
-
-    def first(h, carry):
-        for j in range(4):
-            p = prob[h, j]
-            pbuf[j] = p.astype(bf16)
-            dbuf[j] = score_grad(0, h, j, p)
+
+    def first(h, carry, side):
+        dbuf[h, side] = score_grad(prob[h, side], prob_grad(0, h, side))
+        return carry
+
+    def first_last(h, carry):
+        first(h, carry, 1 - own_side)
         head_back(0, h)
         return carry
 
-    lax.fori_loop(0, OWN, first, 0)
+    g_copy(0).wait_recv()
+    lax.fori_loop(0, OWN, functools.partial(first, side=own_side), 0)
+    g_copy(1).wait_recv()
+    g_copy(2).wait_recv()
+    lax.fori_loop(0, OWN, first_last, 0)
     grad0 = packed_back(0, c_in * noisy_t[...], stream1[...])
     weight = misfit_t[...] * misfit_scale
     out_v[1] = (c_skip * weight + c_in * grad0).T.astype(bf16)
@@ -504,7 +608,6 @@
             relay_copy(b, k).wait_send()
         for m in range(3):
             o_copy(b, m).wait_send()
-            g_copy(b, m).wait_send()
 
         def leave(h, carry, b=b):
             for m in range(3):
@@ -512,11 +615,32 @@
             return carry
 
         lax.fori_loop(0, OWN, leave, 0)
+    for m in range(3):
+        g_copy(m).wait_send()
+        misfit_copy(m).wait_send()
     for stage in range(len(red_peers)):
         for k in range(len(red_peers[stage])):
             red_copy(stage, k).wait_send()
     den_out.wait()
     gui_out.wait()
+
+
+def copy_pair(den, gui, den_out, gui_out, den_v, gui_v, sem):
+    into = [
+        pltpu.make_async_copy(den, den_v, sem.at[0]),
+        pltpu.make_async_copy(gui, gui_v, sem.at[1]),
+    ]
+    away = [
+        pltpu.make_async_copy(den_v, den_out, sem.at[2]),
+        pltpu.make_async_copy(gui_v, gui_out, sem.at[3]),
+    ]
+    for copy in into:
+        copy.start()
+    for i in range(2):
+        into[i].wait()
+        away[i].start()
+    for copy in away:
+        copy.wait()
 
 
 def local(n_shot, n_rec, noisy, misfit, timestep, segment_ids, w_qkv, w_out):
@@ -526,7 +650,6 @@
     scalars = pl.BlockSpec(memory_space=pltpu.SMEM)
     dma = pltpu.SemaphoreType.DMA
     scratch = [
-        pltpu.VMEM((TOK, D), bf16),
         pltpu.VMEM((TOK, D), bf16),
         pltpu.VMEM((D, TOK), f32),
         pltpu.VMEM((D, TOK), f32),
@@ -538,18 +661,21 @@
         pltpu.VMEM((2, 3 * TOK, D), bf16),
         pltpu.VMEM((2, D, D), bf16),
         pltpu.VMEM((2, 4, D, TOK), bf16),
+        pltpu.VMEM((4, TOK, D), bf16),
         pltpu.VMEM((2, OWN, 4, 3 * HS, TOK), bf16),
         pltpu.VMEM((2, OWN, 4, 3 * HS, TOK), bf16),
         pltpu.VMEM((2, OWN, 4, 3 * HS, TOK), bf16),
         pltpu.VMEM((2, OWN, 4, TOK, 8 * HS), bf16),
         pltpu.VMEM((2, OWN, 4, TOK, 4 * HS), bf16),
-        pltpu.VMEM((2, 4, 4 * TOK, TOK), f32),
-        pltpu.VMEM((OWN, 4, 4 * TOK, TOK), f32),
-        pltpu.VMEM((4, 4 * TOK, TOK), bf16),
-        pltpu.VMEM((4, 4 * TOK, TOK), bf16),
+        pltpu.VMEM((2, 4, GROUPS, TOK), bf16),
+        pltpu.VMEM((OWN, 2, 4 * TOK, 2 * TOK), f32),
+        pltpu.VMEM((2, OWN, 2, 4 * TOK, 2 * TOK), bf16),
+        pltpu.VMEM((OWN, 2, 4 * TOK, 2 * TOK), bf16),
+        pltpu.VMEM((2, 4 * TOK, 2 * TOK), f32),
+        pltpu.VMEM((2, 4 * TOK, 2 * TOK), f32),
         pltpu.VMEM((2, 4, TOK, TOK), bf16),
         pltpu.VMEM((2, 4, TOK, TOK), bf16),
-        pltpu.VMEM((2, 4, TOK, TOK), bf16),
+        pltpu.VMEM((4, TOK, TOK), bf16),
         pltpu.VMEM((2, 4, TOK, TOK), bf16),
         pltpu.VMEM((2, OWN, 4, 3 * HS, TOK), bf16),
         pltpu.VMEM((2, 4, OWN, 3 * HS, TOK), bf16),
@@ -564,10 +690,12 @@
         dma((2, CHUNKS)),
         dma((2, CHUNKS)),
         dma((2, CHUNKS)),
+        dma((3,)),
+        dma((3,)),
         dma((2, 3)),
         dma((2, 3)),
-        dma((2, 3)),
-        dma((2, 3)),
+        dma((3,)),
+        dma((3,)),
         dma((2, 3, OWN)),
         dma((2, 3, OWN)),
         dma((len(stages) + 1, 3)),
@@ -580,13 +708,22 @@
         out_specs=[any_space, any_space],
         scratch_shapes=scratch,
         compiler_params=pltpu.CompilerParams(
-            collective_id=0, has_side_effects=True, vmem_limit_bytes=62 * 1024 * 1024
+            collective_id=0, has_side_effects=True, vmem_limit_bytes=VMEM_LIMIT
         ),
         cost_estimate=pl.CostEstimate(
             flops=2_000_000_000, bytes_accessed=6_000_000, transcendentals=2_000_000
         ),
         name="window_pair",
     )(noisy.reshape(TOK, D), misfit.reshape(TOK, D), timestep, segment_ids, w_qkv, w_out)
+    den, gui = pl.pallas_call(
+        copy_pair,
+        out_shape=[jax.ShapeDtypeStruct((TOK, D), bf16)] * 2,
+        in_specs=[any_space, any_space],
+        out_specs=[any_space, any_space],
+        scratch_shapes=[pltpu.VMEM((TOK, D), bf16), pltpu.VMEM((TOK, D), bf16), dma((4,))],
+        compiler_params=pltpu.CompilerParams(vmem_limit_bytes=VMEM_LIMIT),
+        name="copy_pair",
+    )(den, gui)
     return den.reshape(shape), gui.reshape(shape)
 
 

time: 87.4 us -> 79.2 us (0.906)
  Pallas kernels: 82.8 us -> 77.7 us
  local copies, waits for them, and re-layouts: 3.14 us -> 0 us
    pallas_call x1, Pallas kernels: 82.8 us -> 76.1 us  [local(): pl.pallas_call(functools.partial(kernel, n_shot, n_rec, stages), out_shap...]
    unnamed x2 -> x0, local copies, waits for them, and re-layouts: 3.14 us -> none
    pallas_call x0 -> x1, Pallas kernels: none -> 1.66 us  [local(): pl.pallas_call(copy_pair, out_shape=[jax.ShapeDtypeStruct((TOK, D), bf16)...]
where the time goes in v2:
time: 79.2 us; the launch traced here: 79 us
  Pallas kernels  77.7 us (98%)
  between operations  1.28 us (2%)
    pallas_call x1, Pallas kernels, local(): pl.pallas_call(functools.partial(kernel, n_shot, n_rec, stages), out_shap...  76.1 us
    pallas_call x1, Pallas kernels, local(): pl.pallas_call(copy_pair, out_shape=[jax.ShapeDtypeStruct((TOK, D), bf16)...  1.66 us

profile of v2, /device:TPU:48, one launch (start us, length us, event | category | flops | bytes accessed | tf_op | source)
XLA Modules:
  0.0 79.0 jit_solution(7847731412756684272)
XLA Ops:
  1.3 76.1 %window_pair.1 = (bf16[128,512]{1,0:T(8,128)(2,1)}, bf16[128,512]{1,0:T(8,128)(2,1)}) custom-call(bf16[128,512]{1,0:T(8,128)(2,1)} %bitcast.4, bf16[128,512]{1,0:T(8,128)(2,1)} %bitcast.5, s32[1]{0:T(128)S(6)} %copy.8.timestep, s32[256]{0:T(256)} %segs.1, bf16[2,512,1536]{2,1,0:T(8,128)(2,1)} %w_qkv.1, bf16[2,512,512]{2,1,0:T(8,128)(2,1)} %w_out.1), custom_call_target="tpu_custom_call" | custom-call | flops 2000000000 | bytes 6000000 | tf_op jit(solution)/shard_map/window_pair/pallas_call | solution.py:704
  77.4 1.7 %copy_pair.1 = (bf16[128,512]{1,0:T(8,128)(2,1)}, bf16[128,512]{1,0:T(8,128)(2,1)}) custom-call(bf16[128,512]{1,0:T(8,128)(2,1)} %get-tuple-element.6.den, bf16[128,512]{1,0:T(8,128)(2,1)} %get-tuple-element.7.gui), custom_call_target="tpu_custom_call" | custom-call | tf_op jit(solution)/shard_map/copy_pair/pallas_call | solution.py:718

commit v3 on v2

--- a/solution.py
+++ b/solution.py
@@ -128,6 +128,7 @@
     noisy_t,
     misfit_t,
     stream1,
+    grad_mid,
     inverse,
     wfull,
     wofull,
@@ -145,8 +146,6 @@
     prob,
     pbuf,
     dbuf,
-    sbuf,
-    tbuf,
     ost,
     obuf,
     gst,
@@ -183,10 +182,6 @@
         own.append(here)
         blocks.append([2 * far + 1 - near, 2 - 2 * far + near, 3 - 2 * far - near])
         peers.append(partners)
-    def block_at(b, i):
-        near, far = places[b][:2]
-        return 2 * (far + (i // 2) * (1 - 2 * far)) + near + (i % 2) * (1 - 2 * near)
-
     red_peers = [peers[0]] + [stage_peers(stage, shot, rec) for stage in stages]
 
     barrier = pltpu.get_barrier_semaphore()
@@ -227,43 +222,72 @@
 
     def far_copy(b, k):
         block = nbuf.at[b, own[b], pl.ds(k * rows, rows)]
-        return remote(block, block, far_s.at[b, k], far_r.at[b, k], peers[b][1])
+        return remote(block, block, far_s.at[b], far_r.at[b, k], peers[b][1])
+
+    def far_sent(b):
+        block = nbuf.at[b, own[b]]
+        remote(block, block, far_s.at[b], far_r.at[b, 0], peers[b][1]).wait_send()
 
     def relay_copy(b, k):
         block = nbuf.at[b, blocks[b][1], pl.ds(k * rows, rows)]
-        return remote(block, block, rel_s.at[b, k], rel_r.at[b, k], peers[b][0])
+        return remote(block, block, rel_s.at[b], rel_r.at[b], peers[b][0])
+
+    def relay_all(b):
+        source, arrived = nbuf.at[b, blocks[b][1]], nbuf.at[b, blocks[b][2]]
+        return remote(source, arrived, rel_s.at[b], rel_r.at[b], peers[b][0])
 
     def misfit_copy(m):
         block = mbuf.at[blocks[1][1] if m == 2 else own[1]]
-        return remote(block, block, mis_s.at[m], mis_r.at[m], peers[1][m % 2])
+        return remote(block, block, mis_s.at[0], mis_r.at[m], peers[1][m % 2])
+
+    def misfit_sent():
+        block = mbuf.at[pl.ds(0, 3)]
+        remote(block, block, mis_s.at[0], mis_r.at[0], peers[1][0]).wait_send()
 
     def o_copy(b, m):
         return remote(
-            ost.at[b, blocks[b][m]], obuf.at[b, own[b]], o_s.at[b, m], o_r.at[b, m], peers[b][m]
+            ost.at[b, blocks[b][m]], obuf.at[b, own[b]], o_s.at[b], o_r.at[b], peers[b][m]
         )
+
+    def o_all(b):
+        source, arrived = ost.at[b, pl.ds(0, 3)], obuf.at[b, pl.ds(0, 3)]
+        return remote(source, arrived, o_s.at[b], o_r.at[b], peers[b][0])
 
     def g_copy(m):
         return remote(
-            gst.at[blocks[0][m]], gbuf.at[0, own[0]], g_s.at[m], g_r.at[m], peers[0][m]
+            gst.at[blocks[0][m]], gbuf.at[0, own[0]], g_s.at[0], g_r.at[m], peers[0][m]
         )
+
+    def g_sent():
+        source, arrived = gst.at[pl.ds(0, 3)], gbuf.at[0, pl.ds(0, 3)]
+        remote(source, arrived, g_s.at[0], g_r.at[0], peers[0][0]).wait_send()
 
     def gp_copy(b, m, h):
         return remote(
             gpst.at[b, h, blocks[b][m]],
             gpbuf.at[b, own[b], h],
-            gp_s.at[b, m, h],
-            gp_r.at[b, m, h],
+            gp_s.at[b, m],
+            gp_r.at[b, m],
             peers[b][m],
         )
+
+    def gp_all(b, m):
+        source, arrived = gpst.at[b, :, blocks[b][m]], gpbuf.at[b, blocks[b][m]]
+        return remote(source, arrived, gp_s.at[b, m], gp_r.at[b, m], peers[b][m])
 
     def red_copy(stage, k):
         return remote(
             part.at[stage, 0],
             part.at[stage, k + 1],
-            red_s.at[stage, k],
-            red_r.at[stage, k],
+            red_s.at[stage],
+            red_r.at[stage],
             red_peers[stage][k],
         )
+
+    def red_all(stage):
+        peers_of = red_peers[stage]
+        block = part.at[stage, pl.ds(1, len(peers_of))]
+        return remote(block, block, red_s.at[stage], red_r.at[stage], peers_of[0])
 
     def red_send(stage, value):
         part[stage, 0] = value
@@ -271,9 +295,9 @@
             red_copy(stage, k).start()
 
     def red_take(stage):
+        red_all(stage).wait_recv()
         total = part[stage, 0]
         for k in range(len(red_peers[stage])):
-            red_copy(stage, k).wait_recv()
             total = total + part[stage, k + 1]
         return total
 
@@ -344,9 +368,9 @@
             far_copy(b, k).wait_recv()
             relay_copy(b, k).start()
 
-    def relayed(b):
-        for k in range(CHUNKS):
-            relay_copy(b, k).wait_recv()
+    def gather_last(b):
+        relay_all(b).wait_recv()
+        project(b, blocks[b][2])
 
     def scores_of(b, h, side):
         parts = []
@@ -392,24 +416,21 @@
         for m in (2, 1, 0):
             gp_copy(b, m, h).start()
         gpbuf[b, own[b], h] = gpst[b, h, own[b]]
-        if b == 1:
-            o = fold3(dot(wide(v3, b, h), pw)).astype(bf16)
-            for j in range(4):
-                ost[b, j, head_rows(h), :] = o[:, j * TOK : (j + 1) * TOK]
 
     def packed_back(b, stream, grad_next):
-        def arrive(h, carry):
-            for m in range(3):
-                gp_copy(b, m, h).wait_recv()
-            return carry
-
-        lax.fori_loop(0, OWN, arrive, 0)
-        pieces = []
-        for third in range(3):
-            for i in range(4):
-                for h in range(OWN):
-                    pieces.append(gpbuf[b, i, h, third * HS : (third + 1) * HS, :])
-        grad_normed = dot(wfull[b], jnp.concatenate(pieces, axis=0))
+        own_side = own[b] // 2
+        grad_normed = None
+        for side, arrivals in ((own_side, (0,)), (1 - own_side, (1, 2))):
+            for m in arrivals:
+                gp_all(b, m).wait_recv()
+            for third in range(3):
+                pieces = []
+                for i in range(2):
+                    for h in range(OWN):
+                        pieces.append(gpbuf[b, 2 * side + i, h, third * HS : (third + 1) * HS, :])
+                at = pl.multiple_of(third * D + side * 2 * TOK, TOK)
+                some = dot(wfull[b, :, pl.ds(at, 2 * TOK)], jnp.concatenate(pieces, axis=0))
+                grad_normed = some if grad_normed is None else grad_normed + some
         inv = inverse[b]
         normed = stream * inv
         mean = jnp.sum(grad_normed * normed, axis=0, keepdims=True) * (1.0 / D)
@@ -430,10 +451,6 @@
 
     def branch(b):
         return dot(wot[b], obuf[b].reshape(D, TOK))
-
-    def forward(stage):
-        if stage < len(stages):
-            red_send(stage + 1, red_take(stage))
 
     gather_start(0)
     misfit_in.wait()
@@ -443,128 +460,101 @@
     squares = jnp.sum(misfit_f * misfit_f, axis=0, keepdims=True)
     squares = squares[:, :128] + squares[:, 128:256] + squares[:, 256:384] + squares[:, 384:]
     red_send(0, jnp.broadcast_to(squares, (8, 128)))
-    out_in[0].start()
+    for copy in out_in + col_in[1]:
+        copy.start()
     prepare_weights(0)
-
-    def project_first(i, carry):
-        @pl.when(i == 1)
-        def _():
-            make_mask(0)
-            misfit_t[...] = mbuf[own[1]].astype(f32).T
-            relay(0)
-            near_copy(0).wait_recv()
-            out_in[1].start()
-            for copy in col_in[1]:
-                copy.start()
-
-        @pl.when(i == 2)
-        def _():
-            forward(0)
-
-        @pl.when(i == 3)
-        def _():
-            out_in[0].wait()
-            wot[0] = wofull[0].T
-            relayed(0)
-
-        project(0, block_at(0, i))
-        return carry
-
-    lax.fori_loop(0, 4, project_first, 0)
+    project(0, own[0])
+    make_mask(0)
+    misfit_t[...] = misfit_f.T
+    near_copy(0).wait_recv()
+    project(0, blocks[0][0])
+    relay(0)
+    red_send(1, red_take(0))
+    project(0, blocks[0][1])
+    for b in range(2):
+        out_in[b].wait()
+    wot[0] = wofull[0].T
+    gather_last(0)
+    takes = list(range(1, len(stages)))
+
+    def next_stage():
+        if takes:
+            stage = takes.pop(0)
+            red_send(stage + 1, red_take(stage))
+
     own_side = own[0] // 2
-
-    def first_place(i):
-        return i % OWN, own_side + (1 - i // OWN) * (1 - 2 * own_side)
-
-    sbuf[0] = scores_of(0, *first_place(0))
-
-    def first_ahead(i, carry):
-        h, side = first_place(i)
-        sbuf[(i + 1) % 2] = scores_of(0, *first_place((i + 1) % (2 * OWN)))
-        p = softmax(sbuf[i % 2])
+    order = [(side, h) for side in (1 - own_side, own_side) for h in range(OWN)]
+    scores = [scores_of(0, order[0][1], order[0][0])]
+    for at, (side, h) in enumerate(order):
+        if at + 1 < len(order):
+            scores.append(scores_of(0, order[at + 1][1], order[at + 1][0]))
+        p = softmax(scores.pop(0))
         prob[h, side] = p
         p = p.astype(bf16)
         pbuf[0, h, side] = p
         o = fold3(dot(wide(v3, 0, h), p)).astype(bf16)
-        for j in range(2):
-            ost[0, 2 * side + j, head_rows(h), :] = o[:, j * TOK : (j + 1) * TOK]
-
-        @pl.when(i == 1)
-        def _():
-            forward(1)
-
-        @pl.when(i == 3)
-        def _():
+        for i in range(2):
+            ost[0, 2 * side + i, h * HS : (h + 1) * HS, :] = o[:, i * TOK : (i + 1) * TOK]
+        if at == 1 or at == 5:
+            next_stage()
+        if at == 3:
             o_copy(0, 2).start()
             o_copy(0, 1).start()
             misfit_copy(1).wait_recv()
             misfit_copy(2).start()
-
-        @pl.when(i == 5)
-        def _():
-            forward(2)
-
-        return carry
-
-    lax.fori_loop(0, 2 * OWN, first_ahead, 0)
     o_copy(0, 0).start()
     obuf[0, own[0]] = ost[0, own[0]]
     prepare_weights(1)
-    forward(3)
-    for m in range(3):
-        o_copy(0, m).wait_recv()
+    next_stage()
+    o_all(0).wait_recv()
     stream1[...] = c_in * noisy_t[...] + branch(0)
     normalise(1, stream1[...])
 
     gather_start(1)
+    full_in[1].start()
+    full_in[0].start()
+    project(1, own[1])
     make_mask(1)
-    full_in[1].start()
+    while takes:
+        next_stage()
     square_sum = jnp.sum(red_take(len(stages))[:1], axis=1, keepdims=True)
     entries = float(n_shot * n_rec * TOK * D)
     misfit_scale = lax.rsqrt(square_sum / entries + norm_eps)
-    out_in[1].wait()
+    near_copy(1).wait_recv()
+    project(1, blocks[1][0])
+    second_grads(own[1])
     misfit_copy(0).wait_recv()
+    second_grads(blocks[1][0])
+    second_grads(blocks[1][1])
     misfit_copy(2).wait_recv()
-
-    def project_second(i, carry):
-        @pl.when(i == 1)
-        def _():
-            near_copy(1).wait_recv()
-
-        @pl.when(i == 2)
-        def _():
-            relay(1)
-
-        @pl.when(i == 3)
-        def _():
-            wot[1] = wofull[1].T
-            full_in[0].start()
-            relayed(1)
-
-        second_grads(block_at(1, i))
-        project(1, block_at(1, i))
+    second_grads(blocks[1][2])
+    relay(1)
+    project(1, blocks[1][1])
+    wot[1] = wofull[1].T
+    gather_last(1)
+
+    def second(pair, carry):
+        todo = [(2 * pair + u, side) for u in range(2) for side in range(2)]
+        ahead = [(scores_of(1, *at), prob_grad(1, *at)) for at in todo[:2]]
+        for step, (h, side) in enumerate(todo):
+            scores, grad_prob = ahead.pop(0)
+            p = softmax(scores)
+            pbuf[1, h, side] = p.astype(bf16)
+            dbuf[h, side] = score_grad(p, grad_prob)
+            if step + 2 < len(todo):
+                at = todo[step + 2]
+                ahead.append((scores_of(1, *at), prob_grad(1, *at)))
+            if side == 1:
+                head_back(1, h)
         return carry
 
-    lax.fori_loop(0, 4, project_second, 0)
-    sbuf[0] = scores_of(1, 0, 0)
-    tbuf[0] = prob_grad(1, 0, 0)
-
-    def second(i, carry):
-        h, side = i // 2, i % 2
-        later = (i + 1) % (2 * OWN)
-        sbuf[(i + 1) % 2] = scores_of(1, later // 2, later % 2)
-        tbuf[(i + 1) % 2] = prob_grad(1, later // 2, later % 2)
-        p = softmax(sbuf[i % 2])
-        pbuf[1, h, side] = p.astype(bf16)
-        dbuf[h, side] = score_grad(p, tbuf[i % 2])
-
-        @pl.when(side == 1)
-        def _():
-            head_back(1, h)
-
-        return carry
-
-    lax.fori_loop(0, 2 * OWN, second, 0)
+    lax.fori_loop(0, OWN // 2, second, 0)
+
+    for h in range(OWN):
+        for side in range(2):
+            o = fold3(dot(wide(v3, 1, h), pbuf[1, h, side])).astype(bf16)
+            for i in range(2):
+                ost[1, 2 * side + i, h * HS : (h + 1) * HS, :] = o[:, i * TOK : (i + 1) * TOK]
     for m in (2, 1, 0):
         o_copy(1, m).start()
     obuf[1, own[1]] = ost[1, own[1]]
@@ -573,54 +563,51 @@
     weight = misfit_t[...] * misfit_scale
     grad1 = packed_back(1, stream1[...], c_out * weight)
     send_grads(grad1)
-    for m in range(3):
-        o_copy(1, m).wait_recv()
+    grad_mid[...] = grad1
+
+    def first(pair, carry, side):
+        todo = [2 * pair + u for u in range(2)]
+        grad_probs = [prob_grad(0, h, side) for h in todo]
+        for h, grad_prob in zip(todo, grad_probs):
+            dbuf[h, side] = score_grad(prob[h, side], grad_prob)
+        return carry
+
+    def first_last(pair, carry):
+        first(pair, carry, 1 - own_side)
+        for u in range(2):
+            head_back(0, 2 * pair + u)
+        return carry
+
+    g_copy(0).wait_recv()
+    lax.fori_loop(0, OWN // 2, functools.partial(first, side=own_side), 0)
+    g_copy(1).wait_recv()
+    g_copy(2).wait_recv()
+    lax.fori_loop(0, OWN // 2, first_last, 0)
+
+    o_all(1).wait_recv()
     final = stream1[...] + branch(1)
     out_v[0] = (c_skip * noisy_t[...] + c_out * final).T.astype(bf16)
     den_out = pltpu.make_async_copy(out_v.at[0], den, out_sem.at[0])
     den_out.start()
-    stream1[...] = grad1
-
-    def first(h, carry, side):
-        dbuf[h, side] = score_grad(prob[h, side], prob_grad(0, h, side))
-        return carry
-
-    def first_last(h, carry):
-        first(h, carry, 1 - own_side)
-        head_back(0, h)
-        return carry
-
-    g_copy(0).wait_recv()
-    lax.fori_loop(0, OWN, functools.partial(first, side=own_side), 0)
-    g_copy(1).wait_recv()
-    g_copy(2).wait_recv()
-    lax.fori_loop(0, OWN, first_last, 0)
-    grad0 = packed_back(0, c_in * noisy_t[...], stream1[...])
+    for b in range(2):
+        near_copy(b).wait_send()
+        far_sent(b)
+        relay_all(b).wait_send()
+        o_all(b).wait_send()
+    g_sent()
+    misfit_sent()
+    for stage in range(len(red_peers)):
+        red_all(stage).wait_send()
+    for m in range(3):
+        gp_all(1, m).wait_send()
+    grad0 = packed_back(0, c_in * noisy_t[...], grad_mid[...])
     weight = misfit_t[...] * misfit_scale
     out_v[1] = (c_skip * weight + c_in * grad0).T.astype(bf16)
     gui_out = pltpu.make_async_copy(out_v.at[1], gui, out_sem.at[1])
     gui_out.start()
 
-    for b in range(2):
-        near_copy(b).wait_send()
-        for k in range(CHUNKS):
-            far_copy(b, k).wait_send()
-            relay_copy(b, k).wait_send()
-        for m in range(3):
-            o_copy(b, m).wait_send()
-
-        def leave(h, carry, b=b):
-            for m in range(3):
-                gp_copy(b, m, h).wait_send()
-            return carry
-
-        lax.fori_loop(0, OWN, leave, 0)
     for m in range(3):
-        g_copy(m).wait_send()
-        misfit_copy(m).wait_send()
-    for stage in range(len(red_peers)):
-        for k in range(len(red_peers[stage])):
-            red_copy(stage, k).wait_send()
+        gp_all(0, m).wait_send()
     den_out.wait()
     gui_out.wait()
 
@@ -651,6 +638,7 @@
     dma = pltpu.SemaphoreType.DMA
     scratch = [
         pltpu.VMEM((TOK, D), bf16),
+        pltpu.VMEM((D, TOK), f32),
         pltpu.VMEM((D, TOK), f32),
         pltpu.VMEM((D, TOK), f32),
         pltpu.VMEM((D, TOK), f32),
@@ -671,8 +659,6 @@
         pltpu.VMEM((OWN, 2, 4 * TOK, 2 * TOK), f32),
         pltpu.VMEM((2, OWN, 2, 4 * TOK, 2 * TOK), bf16),
         pltpu.VMEM((OWN, 2, 4 * TOK, 2 * TOK), bf16),
-        pltpu.VMEM((2, 4 * TOK, 2 * TOK), f32),
-        pltpu.VMEM((2, 4 * TOK, 2 * TOK), f32),
         pltpu.VMEM((2, 4, TOK, TOK), bf16),
         pltpu.VMEM((2, 4, TOK, TOK), bf16),
         pltpu.VMEM((4, TOK, TOK), bf16),
@@ -686,20 +672,20 @@
         dma((2,)),
         dma((2,)),
         dma((2,)),
+        dma((2,)),
         dma((2, CHUNKS)),
-        dma((2, CHUNKS)),
-        dma((2, CHUNKS)),
-        dma((2, CHUNKS)),
+        dma((2,)),
+        dma((2,)),
+        dma((1,)),
         dma((3,)),
+        dma((2,)),
+        dma((2,)),
+        dma((1,)),
         dma((3,)),
         dma((2, 3)),
         dma((2, 3)),
-        dma((3,)),
-        dma((3,)),
-        dma((2, 3, OWN)),
-        dma((2, 3, OWN)),
-        dma((len(stages) + 1, 3)),
-        dma((len(stages) + 1, 3)),
+        dma((len(stages) + 1,)),
+        dma((len(stages) + 1,)),
     ]
     den, gui = pl.pallas_call(
         functools.partial(kernel, n_shot, n_rec, stages),

time: 79.2 us -> 76.3 us (0.963)
  Pallas kernels: 77.7 us -> 74.8 us
    pallas_call x1, Pallas kernels: 76.1 us -> 73.2 us  [local(): pl.pallas_call(functools.partial(kernel, n_shot, n_rec, stages), out_shap...]
where the time goes in v3:
time: 76.3 us; the launch traced here: 76.1 us
  Pallas kernels  74.8 us (98%)
  between operations  1.28 us (2%)
    pallas_call x1, Pallas kernels, local(): pl.pallas_call(functools.partial(kernel, n_shot, n_rec, stages), out_shap...  73.2 us
    pallas_call x1, Pallas kernels, local(): pl.pallas_call(copy_pair, out_shape=[jax.ShapeDtypeStruct((TOK, D), bf16)...  1.66 us

profile of v3, /device:TPU:48, one launch (start us, length us, event | category | flops | bytes accessed | tf_op | source)
XLA Modules:
  0.0 76.1 jit_solution(823311620209014839)
XLA Ops:
  1.3 73.2 %window_pair.1 = (bf16[128,512]{1,0:T(8,128)(2,1)}, bf16[128,512]{1,0:T(8,128)(2,1)}) custom-call(bf16[128,512]{1,0:T(8,128)(2,1)} %bitcast.4, bf16[128,512]{1,0:T(8,128)(2,1)} %bitcast.5, s32[1]{0:T(128)S(6)} %copy.8.timestep, s32[256]{0:T(256)} %segs.1, bf16[2,512,1536]{2,1,0:T(8,128)(2,1)} %w_qkv.1, bf16[2,512,512]{2,1,0:T(8,128)(2,1)} %w_out.1), custom_call_target="tpu_custom_call" | custom-call | flops 2000000000 | bytes 6000000 | tf_op jit(solution)/shard_map/window_pair/pallas_call | solution.py:690
  74.5 1.7 %copy_pair.1 = (bf16[128,512]{1,0:T(8,128)(2,1)}, bf16[128,512]{1,0:T(8,128)(2,1)}) custom-call(bf16[128,512]{1,0:T(8,128)(2,1)} %get-tuple-element.6.den, bf16[128,512]{1,0:T(8,128)(2,1)} %get-tuple-element.7.gui), custom_call_target="tpu_custom_call" | custom-call | tf_op jit(solution)/shard_map/copy_pair/pallas_call | solution.py:704

commit v4 on v3

--- a/solution.py
+++ b/solution.py
@@ -33,13 +33,13 @@
 
 
 def reduction_stages(n_shot, n_rec):
-    digits = []
-    for axis, size in ((0, n_shot), (1, n_rec)):
-        stride = 2
-        while stride < size:
-            digits.append((axis, stride, 2))
-            stride *= 2
-    return [digits[i : i + 2] for i in range(0, len(digits), 2)]
+    stages = [
+        [(1, 1, min(n_rec, 4)), (0, 1, 2)],
+        [(0, 16, n_shot // 16), (1, 4, n_rec // 4)],
+        [(0, 2, min(n_shot // 2, 8))],
+    ]
+    stages = [[digit for digit in stage if digit[2] > 1] for stage in stages]
+    return [stage for stage in stages if stage]
 
 
 def stage_peers(stage, shot, rec):
@@ -182,10 +182,10 @@
         own.append(here)
         blocks.append([2 * far + 1 - near, 2 - 2 * far + near, 3 - 2 * far - near])
         peers.append(partners)
-    red_peers = [peers[0]] + [stage_peers(stage, shot, rec) for stage in stages]
+    red_peers = [stage_peers(stage, shot, rec) for stage in stages]
 
     barrier = pltpu.get_barrier_semaphore()
-    greeted = peers[0] + peers[1] + [peer for some in red_peers[1:] for peer in some]
+    greeted = peers[0] + peers[1] + [peer for some in red_peers for peer in some]
     for peer in greeted:
         pl.semaphore_signal(barrier, inc=1, device_id=peer, device_id_type=MESH)
 
@@ -452,6 +452,10 @@
     def branch(b):
         return dot(wot[b], obuf[b].reshape(D, TOK))
 
+    def forward(stage):
+        if stage + 1 < len(stages):
+            red_send(stage + 1, red_take(stage))
+
     gather_start(0)
     misfit_in.wait()
     misfit_copy(1).start()
@@ -469,19 +473,12 @@
     near_copy(0).wait_recv()
     project(0, blocks[0][0])
     relay(0)
-    red_send(1, red_take(0))
+    forward(0)
     project(0, blocks[0][1])
     for b in range(2):
         out_in[b].wait()
     wot[0] = wofull[0].T
     gather_last(0)
-    takes = list(range(1, len(stages)))
-
-    def next_stage():
-        if takes:
-            stage = takes.pop(0)
-            red_send(stage + 1, red_take(stage))
-
     own_side = own[0] // 2
     order = [(side, h) for side in (1 - own_side, own_side) for h in range(OWN)]
     scores = [scores_of(0, order[0][1], order[0][0])]
@@ -495,17 +492,16 @@
         o = fold3(dot(wide(v3, 0, h), p)).astype(bf16)
         for i in range(2):
             ost[0, 2 * side + i, h * HS : (h + 1) * HS, :] = o[:, i * TOK : (i + 1) * TOK]
-        if at == 1 or at == 5:
-            next_stage()
+        if at == 4:
+            forward(1)
         if at == 3:
             o_copy(0, 2).start()
             o_copy(0, 1).start()
-            misfit_copy(1).wait_recv()
-            misfit_copy(2).start()
     o_copy(0, 0).start()
     obuf[0, own[0]] = ost[0, own[0]]
     prepare_weights(1)
-    next_stage()
+    misfit_copy(1).wait_recv()
+    misfit_copy(2).start()
     o_all(0).wait_recv()
     stream1[...] = c_in * noisy_t[...] + branch(0)
     normalise(1, stream1[...])
@@ -515,13 +511,11 @@
     full_in[0].start()
     project(1, own[1])
     make_mask(1)
-    while takes:
-        next_stage()
-    square_sum = jnp.sum(red_take(len(stages))[:1], axis=1, keepdims=True)
+    near_copy(1).wait_recv()
+    project(1, blocks[1][0])
+    square_sum = jnp.sum(red_take(len(stages) - 1)[:1], axis=1, keepdims=True)
     entries = float(n_shot * n_rec * TOK * D)
     misfit_scale = lax.rsqrt(square_sum / entries + norm_eps)
-    near_copy(1).wait_recv()
-    project(1, blocks[1][0])
     second_grads(own[1])
     misfit_copy(0).wait_recv()
     second_grads(blocks[1][0])
@@ -665,7 +659,7 @@
         pltpu.VMEM((2, 4, TOK, TOK), bf16),
         pltpu.VMEM((2, OWN, 4, 3 * HS, TOK), bf16),
         pltpu.VMEM((2, 4, OWN, 3 * HS, TOK), bf16),
-        pltpu.VMEM((len(stages) + 1, 4, 8, 128), f32),
+        pltpu.VMEM((len(stages), 8, 8, 128), f32),
         pltpu.VMEM((2, TOK, D), bf16),
         dma((2,)),
         dma((10,)),
@@ -684,8 +678,8 @@
         dma((3,)),
         dma((2, 3)),
         dma((2, 3)),
-        dma((len(stages) + 1,)),
-        dma((len(stages) + 1,)),
+        dma((len(stages),)),
+        dma((len(stages),)),
     ]
     den, gui = pl.pallas_call(
         functools.partial(kernel, n_shot, n_rec, stages),

time: 76.3 us -> 72.6 us (0.952)
  Pallas kernels: 74.8 us -> 71.1 us
    pallas_call x1, Pallas kernels: 73.2 us -> 69.5 us  [local(): pl.pallas_call(functools.partial(kernel, n_shot, n_rec, stages), out_shap...]
where the time goes in v4:
time: 72.6 us; the launch traced here: 72.4 us
  Pallas kernels  71.1 us (98%)
  between operations  1.28 us (2%)
    pallas_call x1, Pallas kernels, local(): pl.pallas_call(functools.partial(kernel, n_shot, n_rec, stages), out_shap...  69.5 us
    pallas_call x1, Pallas kernels, local(): pl.pallas_call(copy_pair, out_shape=[jax.ShapeDtypeStruct((TOK, D), bf16)...  1.66 us

profile of v4, /device:TPU:48, one launch (start us, length us, event | category | flops | bytes accessed | tf_op | source)
XLA Modules:
  0.0 72.4 jit_solution(11773792752537567125)
XLA Ops:
  1.3 69.5 %window_pair.1 = (bf16[128,512]{1,0:T(8,128)(2,1)}, bf16[128,512]{1,0:T(8,128)(2,1)}) custom-call(bf16[128,512]{1,0:T(8,128)(2,1)} %bitcast.4, bf16[128,512]{1,0:T(8,128)(2,1)} %bitcast.5, s32[1]{0:T(128)S(6)} %copy.8.timestep, s32[256]{0:T(256)} %segs.1, bf16[2,512,1536]{2,1,0:T(8,128)(2,1)} %w_qkv.1, bf16[2,512,512]{2,1,0:T(8,128)(2,1)} %w_out.1), custom_call_target="tpu_custom_call" | custom-call | flops 2000000000 | bytes 6000000 | tf_op jit(solution)/shard_map/window_pair/pallas_call | solution.py:684
  70.8 1.7 %copy_pair.1 = (bf16[128,512]{1,0:T(8,128)(2,1)}, bf16[128,512]{1,0:T(8,128)(2,1)}) custom-call(bf16[128,512]{1,0:T(8,128)(2,1)} %get-tuple-element.6.den, bf16[128,512]{1,0:T(8,128)(2,1)} %get-tuple-element.7.gui), custom_call_target="tpu_custom_call" | custom-call | tf_op jit(solution)/shard_map/copy_pair/pallas_call | solution.py:698

commit v5 on v4

--- a/solution.py
+++ b/solution.py
@@ -36,7 +36,6 @@
     stages = [
         [(1, 1, min(n_rec, 4)), (0, 1, 2)],
         [(0, 16, n_shot // 16), (1, 4, n_rec // 4)],
-        [(0, 2, min(n_shot // 2, 8))],
     ]
     stages = [[digit for digit in stage if digit[2] > 1] for stage in stages]
     return [stage for stage in stages if stage]
@@ -153,6 +152,8 @@
     gpst,
     gpbuf,
     part,
+    ring_own,
+    ring,
     out_v,
     in_sem,
     w_sem,
@@ -173,6 +174,8 @@
     gp_r,
     red_s,
     red_r,
+    ring_s,
+    ring_r,
 ):
     shot, rec = lax.axis_index("shot"), lax.axis_index("rec")
     places = window_places(shot, rec, n_shot, n_rec)
@@ -183,9 +186,16 @@
         blocks.append([2 * far + 1 - near, 2 - 2 * far + near, 3 - 2 * far - near])
         peers.append(partners)
     red_peers = [stage_peers(stage, shot, rec) for stage in stages]
+    n_z = min(n_shot // 2, 8)
+    steps = n_z // 2
+    at_z = (shot // 2) % n_z
+    ring_peers = [
+        (shot + 2 * ((at_z + 1) % n_z - at_z), rec),
+        (shot + 2 * ((at_z + n_z - 1) % n_z - at_z), rec),
+    ]
 
     barrier = pltpu.get_barrier_semaphore()
-    greeted = peers[0] + peers[1] + [peer for some in red_peers for peer in some]
+    greeted = peers[0] + peers[1] + ring_peers + [peer for some in red_peers for peer in some]
     for peer in greeted:
         pl.semaphore_signal(barrier, inc=1, device_id=peer, device_id_type=MESH)
 
@@ -301,6 +311,21 @@
             total = total + part[stage, k + 1]
         return total
 
+    def ring_copy(t, d):
+        source = ring_own if t == 0 else ring.at[t - 1, d]
+        return remote(source, ring.at[t, d], ring_s.at[t, d], ring_r.at[t, d], ring_peers[d])
+
+    def ring_ways(t):
+        return (0,) if t == steps - 1 else (0, 1)
+
+    def ring_step(t):
+        if t > 0:
+            for d in ring_ways(t - 1) if t <= steps else ():
+                ring_copy(t - 1, d).wait_recv()
+        if t < steps:
+            for d in ring_ways(t):
+                ring_copy(t, d).start()
+
     fraction = jnp.full((1, TOK), timestep[0].astype(f32), f32) / (STEPS - 1)
     noise_level = sigma_low * jnp.exp(fraction * math.log(sigma_high / sigma_low))
     spread = noise_level * noise_level + sigma_data * sigma_data
@@ -403,19 +428,32 @@
         row_dot = jnp.sum(p * grad_prob, axis=0, keepdims=True)
         return (p * (grad_prob - row_dot)).astype(bf16)
 
-    def head_back(b, h):
-        pw = jnp.concatenate([pbuf[b, h, 0], pbuf[b, h, 1]], axis=1)
-        dw = jnp.concatenate([dbuf[h, 0], dbuf[h, 1]], axis=1)
+    def head_back(b, h, side):
+        keys = pl.ds(pl.multiple_of(side * 2 * TOK, TOK), 2 * TOK)
+        pw = jnp.concatenate([pbuf[b, h, 0, keys, :], pbuf[b, h, 1, keys, :]], axis=1)
+        dw = jnp.concatenate([dbuf[h, 0, keys, :], dbuf[h, 1, keys, :]], axis=1)
         g = jnp.concatenate([gbuf[b, i, head_rows(h), :] for i in range(4)], axis=1)
-        grad_q = (fold3(dot(wide(k3, b, h), dw)) * SCALE).astype(bf16)
+        grad_q = (fold3(dot(wide(k3, b, h), dbuf[h, side])) * SCALE).astype(bf16)
         grad_k = (fold3(dot_nt(wide(q3, b, h), dw)) * (1.0 / LOG2E)).astype(bf16)
         grad_v = dot_nt(g, pw).astype(bf16)
-        for j in range(4):
-            at = slice(j * TOK, (j + 1) * TOK)
-            gpst[b, h, j] = jnp.concatenate([grad_q[:, at], grad_k[:, at], grad_v[:, at]], axis=0)
-        for m in (2, 1, 0):
-            gp_copy(b, m, h).start()
-        gpbuf[b, own[b], h] = gpst[b, h, own[b]]
+        for i in range(2):
+            at = slice(i * TOK, (i + 1) * TOK)
+            gpst[b, h, 2 * side + i] = jnp.concatenate(
+                [grad_q[:, at], grad_k[:, at], grad_v[:, at]], axis=0
+            )
+
+    def other_back(b, h):
+        head_back(b, h, 1 - own[b] // 2)
+        gp_copy(b, 2, h).start()
+        gp_copy(b, 1, h).start()
+
+    def own_back(pair, carry, b):
+        for u in range(2):
+            h = 2 * pair + u
+            head_back(b, h, own[b] // 2)
+            gp_copy(b, 0, h).start()
+            gpbuf[b, own[b], h] = gpst[b, h, own[b]]
+        return carry
 
     def packed_back(b, stream, grad_next):
         own_side = own[b] // 2
@@ -493,7 +531,8 @@
         for i in range(2):
             ost[0, 2 * side + i, h * HS : (h + 1) * HS, :] = o[:, i * TOK : (i + 1) * TOK]
         if at == 4:
-            forward(1)
+            ring_own[...] = red_take(len(stages) - 1)
+            ring_step(0)
         if at == 3:
             o_copy(0, 2).start()
             o_copy(0, 1).start()
@@ -502,6 +541,7 @@
     prepare_weights(1)
     misfit_copy(1).wait_recv()
     misfit_copy(2).start()
+    ring_step(1)
     o_all(0).wait_recv()
     stream1[...] = c_in * noisy_t[...] + branch(0)
     normalise(1, stream1[...])
@@ -509,11 +549,18 @@
     gather_start(1)
     full_in[1].start()
     full_in[0].start()
+    ring_step(2)
     project(1, own[1])
     make_mask(1)
+    ring_step(3)
     near_copy(1).wait_recv()
     project(1, blocks[1][0])
-    square_sum = jnp.sum(red_take(len(stages) - 1)[:1], axis=1, keepdims=True)
+    ring_step(4)
+    ring_sum = ring_own[...]
+    for t in range(steps):
+        for d in ring_ways(t):
+            ring_sum = ring_sum + ring[t, d]
+    square_sum = jnp.sum(ring_sum[:1], axis=1, keepdims=True)
     entries = float(n_shot * n_rec * TOK * D)
     misfit_scale = lax.rsqrt(square_sum / entries + norm_eps)
     second_grads(own[1])
@@ -539,10 +586,11 @@
                 at = todo[step + 2]
                 ahead.append((scores_of(1, *at), prob_grad(1, *at)))
             if side == 1:
-                head_back(1, h)
+                other_back(1, h)
         return carry
 
     lax.fori_loop(0, OWN // 2, second, 0)
+    lax.fori_loop(0, OWN // 2, functools.partial(own_back, b=1), 0)
 
     for h in range(OWN):
         for side in range(2):
@@ -569,7 +617,7 @@
     def first_last(pair, carry):
         first(pair, carry, 1 - own_side)
         for u in range(2):
-            head_back(0, 2 * pair + u)
+            other_back(0, 2 * pair + u)
         return carry
 
     g_copy(0).wait_recv()
@@ -577,6 +625,7 @@
     g_copy(1).wait_recv()
     g_copy(2).wait_recv()
     lax.fori_loop(0, OWN // 2, first_last, 0)
+    lax.fori_loop(0, OWN // 2, functools.partial(own_back, b=0), 0)
 
     o_all(1).wait_recv()
     final = stream1[...] + branch(1)
@@ -592,6 +641,9 @@
     misfit_sent()
     for stage in range(len(red_peers)):
         red_all(stage).wait_send()
+    for t in range(steps):
+        for d in ring_ways(t):
+            ring_copy(t, d).wait_send()
     for m in range(3):
         gp_all(1, m).wait_send()
     grad0 = packed_back(0, c_in * noisy_t[...], grad_mid[...])
@@ -660,6 +712,8 @@
         pltpu.VMEM((2, OWN, 4, 3 * HS, TOK), bf16),
         pltpu.VMEM((2, 4, OWN, 3 * HS, TOK), bf16),
         pltpu.VMEM((len(stages), 8, 8, 128), f32),
+        pltpu.VMEM((8, 128), f32),
+        pltpu.VMEM((4, 2, 8, 128), f32),
         pltpu.VMEM((2, TOK, D), bf16),
         dma((2,)),
         dma((10,)),
@@ -680,6 +734,8 @@
         dma((2, 3)),
         dma((len(stages),)),
         dma((len(stages),)),
+        dma((4, 2)),
+        dma((4, 2)),
     ]
     den, gui = pl.pallas_call(
         functools.partial(kernel, n_shot, n_rec, stages),

time: 72.6 us -> 75.2 us (1.036)
  the two profiles are of different devices: /device:TPU:48 before, /device:TPU:22 now
where the time goes in v5:
time: 75.2 us; the launch traced here: 75 us
  Pallas kernels  73.7 us (98%)
  between operations  1.28 us (2%)
    pallas_call x1, Pallas kernels, local(): pl.pallas_call(functools.partial(kernel, n_shot, n_rec, stages), out_shap...  72.1 us
    pallas_call x1, Pallas kernels, local(): pl.pallas_call(copy_pair, out_shape=[jax.ShapeDtypeStruct((TOK, D), bf16)...  1.66 us

profile of v5, /device:TPU:22, one launch (start us, length us, event | category | flops | bytes accessed | tf_op | source)
XLA Modules:
  0.0 75.0 jit_solution(12179869136349696111)
XLA Ops:
  1.3 72.1 %window_pair.1 = (bf16[128,512]{1,0:T(8,128)(2,1)}, bf16[128,512]{1,0:T(8,128)(2,1)}) custom-call(bf16[128,512]{1,0:T(8,128)(2,1)} %bitcast.4, bf16[128,512]{1,0:T(8,128)(2,1)} %bitcast.5, s32[1]{0:T(128)S(6)} %copy.8.timestep, s32[256]{0:T(256)} %segs.1, bf16[2,512,1536]{2,1,0:T(8,128)(2,1)} %w_qkv.1, bf16[2,512,512]{2,1,0:T(8,128)(2,1)} %w_out.1), custom_call_target="tpu_custom_call" | custom-call | flops 2000000000 | bytes 6000000 | tf_op jit(solution)/shard_map/window_pair/pallas_call | solution.py:740
  73.3 1.7 %copy_pair.1 = (bf16[128,512]{1,0:T(8,128)(2,1)}, bf16[128,512]{1,0:T(8,128)(2,1)}) custom-call(bf16[128,512]{1,0:T(8,128)(2,1)} %get-tuple-element.6.den, bf16[128,512]{1,0:T(8,128)(2,1)} %get-tuple-element.7.gui), custom_call_target="tpu_custom_call" | custom-call | tf_op jit(solution)/shard_map/copy_pair/pallas_call | solution.py:754

commit v6 on v4

--- a/solution.py
+++ b/solution.py
@@ -473,12 +473,12 @@
     near_copy(0).wait_recv()
     project(0, blocks[0][0])
     relay(0)
-    forward(0)
     project(0, blocks[0][1])
     for b in range(2):
         out_in[b].wait()
     wot[0] = wofull[0].T
     gather_last(0)
+    forward(0)
     own_side = own[0] // 2
     order = [(side, h) for side in (1 - own_side, own_side) for h in range(OWN)]
     scores = [scores_of(0, order[0][1], order[0][0])]
@@ -492,8 +492,6 @@
         o = fold3(dot(wide(v3, 0, h), p)).astype(bf16)
         for i in range(2):
             ost[0, 2 * side + i, h * HS : (h + 1) * HS, :] = o[:, i * TOK : (i + 1) * TOK]
-        if at == 4:
-            forward(1)
         if at == 3:
             o_copy(0, 2).start()
             o_copy(0, 1).start()
@@ -509,10 +507,13 @@
     gather_start(1)
     full_in[1].start()
     full_in[0].start()
+    forward(1)
     project(1, own[1])
     make_mask(1)
     near_copy(1).wait_recv()
     project(1, blocks[1][0])
+    relay(1)
+    project(1, blocks[1][1])
     square_sum = jnp.sum(red_take(len(stages) - 1)[:1], axis=1, keepdims=True)
     entries = float(n_shot * n_rec * TOK * D)
     misfit_scale = lax.rsqrt(square_sum / entries + norm_eps)
@@ -522,8 +523,6 @@
     second_grads(blocks[1][1])
     misfit_copy(2).wait_recv()
     second_grads(blocks[1][2])
-    relay(1)
-    project(1, blocks[1][1])
     wot[1] = wofull[1].T
     gather_last(1)
 

time: 72.6 us -> 71.5 us (0.985)
  Pallas kernels: 71.1 us -> 70 us
    pallas_call x1, Pallas kernels: 69.5 us -> 68.3 us  [local(): pl.pallas_call(functools.partial(kernel, n_shot, n_rec, stages), out_shap...]
where the time goes in v6:
time: 71.5 us; the launch traced here: 71.3 us
  Pallas kernels  70 us (98%)
  between operations  1.28 us (2%)
    pallas_call x1, Pallas kernels, local(): pl.pallas_call(functools.partial(kernel, n_shot, n_rec, stages), out_shap...  68.3 us
    pallas_call x1, Pallas kernels, local(): pl.pallas_call(copy_pair, out_shape=[jax.ShapeDtypeStruct((TOK, D), bf16)...  1.66 us

profile of v6, /device:TPU:48, one launch (start us, length us, event | category | flops | bytes accessed | tf_op | source)
XLA Modules:
  0.0 71.3 jit_solution(7285343883628693069)
XLA Ops:
  1.3 68.3 %window_pair.1 = (bf16[128,512]{1,0:T(8,128)(2,1)}, bf16[128,512]{1,0:T(8,128)(2,1)}) custom-call(bf16[128,512]{1,0:T(8,128)(2,1)} %bitcast.4, bf16[128,512]{1,0:T(8,128)(2,1)} %bitcast.5, s32[1]{0:T(128)S(6)} %copy.8.timestep, s32[256]{0:T(256)} %segs.1, bf16[2,512,1536]{2,1,0:T(8,128)(2,1)} %w_qkv.1, bf16[2,512,512]{2,1,0:T(8,128)(2,1)} %w_out.1), custom_call_target="tpu_custom_call" | custom-call | flops 2000000000 | bytes 6000000 | tf_op jit(solution)/shard_map/window_pair/pallas_call | solution.py:683
  69.6 1.7 %copy_pair.1 = (bf16[128,512]{1,0:T(8,128)(2,1)}, bf16[128,512]{1,0:T(8,128)(2,1)}) custom-call(bf16[128,512]{1,0:T(8,128)(2,1)} %get-tuple-element.6.den, bf16[128,512]{1,0:T(8,128)(2,1)} %get-tuple-element.7.gui), custom_call_target="tpu_custom_call" | custom-call | tf_op jit(solution)/shard_map/copy_pair/pallas_call | solution.py:697

commit v7 on v6

--- a/solution.py
+++ b/solution.py
@@ -498,8 +498,6 @@
     o_copy(0, 0).start()
     obuf[0, own[0]] = ost[0, own[0]]
     prepare_weights(1)
-    misfit_copy(1).wait_recv()
-    misfit_copy(2).start()
     o_all(0).wait_recv()
     stream1[...] = c_in * noisy_t[...] + branch(0)
     normalise(1, stream1[...])
@@ -510,6 +508,8 @@
     forward(1)
     project(1, own[1])
     make_mask(1)
+    misfit_copy(1).wait_recv()
+    misfit_copy(2).start()
     near_copy(1).wait_recv()
     project(1, blocks[1][0])
     relay(1)
@@ -523,7 +523,6 @@
     second_grads(blocks[1][1])
     misfit_copy(2).wait_recv()
     second_grads(blocks[1][2])
-    wot[1] = wofull[1].T
     gather_last(1)
 
     def second(pair, carry):
@@ -543,6 +542,7 @@
 
     lax.fori_loop(0, OWN // 2, second, 0)
 
+    wot[1] = wofull[1].T
     for h in range(OWN):
         for side in range(2):
             o = fold3(dot(wide(v3, 1, h), pbuf[1, h, side])).astype(bf16)

time: 71.5 us -> 72.1 us (level)
  the two profiles are of different devices: /device:TPU:48 before, /device:TPU:22 now
where the time goes in v7:
time: 72.1 us; the launch traced here: 71.9 us
  Pallas kernels  70.6 us (98%)
  between operations  1.28 us (2%)
    pallas_call x1, Pallas kernels, local(): pl.pallas_call(functools.partial(kernel, n_shot, n_rec, stages), out_shap...  69 us
    pallas_call x1, Pallas kernels, local(): pl.pallas_call(copy_pair, out_shape=[jax.ShapeDtypeStruct((TOK, D), bf16)...  1.66 us

profile of v7, /device:TPU:22, one launch (start us, length us, event | category | flops | bytes accessed | tf_op | source)
XLA Modules:
  0.0 71.9 jit_solution(2075165149854659263)
XLA Ops:
  1.3 69.0 %window_pair.1 = (bf16[128,512]{1,0:T(8,128)(2,1)}, bf16[128,512]{1,0:T(8,128)(2,1)}) custom-call(bf16[128,512]{1,0:T(8,128)(2,1)} %bitcast.4, bf16[128,512]{1,0:T(8,128)(2,1)} %bitcast.5, s32[1]{0:T(128)S(6)} %copy.8.timestep, s32[256]{0:T(256)} %segs.1, bf16[2,512,1536]{2,1,0:T(8,128)(2,1)} %w_qkv.1, bf16[2,512,512]{2,1,0:T(8,128)(2,1)} %w_out.1), custom_call_target="tpu_custom_call" | custom-call | flops 2000000000 | bytes 6000000 | tf_op jit(solution)/shard_map/window_pair/pallas_call | solution.py:683
  70.3 1.7 %copy_pair.1 = (bf16[128,512]{1,0:T(8,128)(2,1)}, bf16[128,512]{1,0:T(8,128)(2,1)}) custom-call(bf16[128,512]{1,0:T(8,128)(2,1)} %get-tuple-element.6.den, bf16[128,512]{1,0:T(8,128)(2,1)} %get-tuple-element.7.gui), custom_call_target="tpu_custom_call" | custom-call | tf_op jit(solution)/shard_map/copy_pair/pallas_call | solution.py:697

commit v8 on v6

--- a/solution.py
+++ b/solution.py
@@ -553,6 +553,14 @@
     obuf[1, own[1]] = ost[1, own[1]]
     for b in (1, 0):
         full_in[b].wait()
+    for b in range(2):
+        near_copy(b).wait_send()
+        far_sent(b)
+        relay_all(b).wait_send()
+    o_all(0).wait_send()
+    misfit_sent()
+    for stage in range(len(red_peers)):
+        red_all(stage).wait_send()
     weight = misfit_t[...] * misfit_scale
     grad1 = packed_back(1, stream1[...], c_out * weight)
     send_grads(grad1)
@@ -582,15 +590,8 @@
     out_v[0] = (c_skip * noisy_t[...] + c_out * final).T.astype(bf16)
     den_out = pltpu.make_async_copy(out_v.at[0], den, out_sem.at[0])
     den_out.start()
-    for b in range(2):
-        near_copy(b).wait_send()
-        far_sent(b)
-        relay_all(b).wait_send()
-        o_all(b).wait_send()
+    o_all(1).wait_send()
     g_sent()
-    misfit_sent()
-    for stage in range(len(red_peers)):
-        red_all(stage).wait_send()
     for m in range(3):
         gp_all(1, m).wait_send()
     grad0 = packed_back(0, c_in * noisy_t[...], grad_mid[...])

time: 71.5 us -> 71.5 us (level)
  no operation moved by 1% of the time
where the time goes in v8:
time: 71.5 us; the launch traced here: 71.3 us
  Pallas kernels  70 us (98%)
  between operations  1.28 us (2%)
    pallas_call x1, Pallas kernels, local(): pl.pallas_call(functools.partial(kernel, n_shot, n_rec, stages), out_shap...  68.3 us
    pallas_call x1, Pallas kernels, local(): pl.pallas_call(copy_pair, out_shape=[jax.ShapeDtypeStruct((TOK, D), bf16)...  1.66 us

profile of v8, /device:TPU:48, one launch (start us, length us, event | category | flops | bytes accessed | tf_op | source)
XLA Modules:
  0.0 71.3 jit_solution(7446012510948061951)
XLA Ops:
  1.3 68.3 %window_pair.1 = (bf16[128,512]{1,0:T(8,128)(2,1)}, bf16[128,512]{1,0:T(8,128)(2,1)}) custom-call(bf16[128,512]{1,0:T(8,128)(2,1)} %bitcast.4, bf16[128,512]{1,0:T(8,128)(2,1)} %bitcast.5, s32[1]{0:T(128)S(6)} %copy.8.timestep, s32[256]{0:T(256)} %segs.1, bf16[2,512,1536]{2,1,0:T(8,128)(2,1)} %w_qkv.1, bf16[2,512,512]{2,1,0:T(8,128)(2,1)} %w_out.1), custom_call_target="tpu_custom_call" | custom-call | flops 2000000000 | bytes 6000000 | tf_op jit(solution)/shard_map/window_pair/pallas_call | solution.py:684
  69.6 1.7 %copy_pair.1 = (bf16[128,512]{1,0:T(8,128)(2,1)}, bf16[128,512]{1,0:T(8,128)(2,1)}) custom-call(bf16[128,512]{1,0:T(8,128)(2,1)} %get-tuple-element.6.den, bf16[128,512]{1,0:T(8,128)(2,1)} %get-tuple-element.7.gui), custom_call_target="tpu_custom_call" | custom-call | tf_op jit(solution)/shard_map/copy_pair/pallas_call | solution.py:698
